TPU v7x, 128 devices: a whole 4x4x4 slice. The times are simulated.
128 devices in a mesh: gx: 16 (over y, x_lo, core), gy: 8 (over x_hi, z).
Axes of the slice: x: 4 (x_hi: 2, x_lo: 2; x = x_hi * 2 + x_lo), y: 4, z: 4, core: 2. Of those that a mesh axis runs over, the one named last changes fastest.
Arguments:
- temp_start: float32 [8, 4096, 4096], P(None, ('gx', 'gy')), may hold values from -6 to 6
- heat_input: float32 [8, 4096, 4096], P(None, ('gx', 'gy')), may hold values from -3 to 3
- lateral: float32 [8], replicated, may hold values from 0.03 to 0.15
- vertical: float32 [7], replicated, may hold values from 0.03 to 0.15
- weighting: float32 [8], replicated, may hold values from -1 to 1
- modulus: float32 [4096, 4096], P('gx', 'gy'), may hold values from 0.3 to 3
- warp_prev: float32 [4096, 4096], P('gx', 'gy'), may hold values from -6 to 6
- joint_cell: int32 [262144], P(('gx', 'gy')), may hold values from 0 to 131071
- joint_owner: int32 [262144, 1], P(('gx', 'gy')), may hold values from 0 to 127; in each aligned block of 2048 rows (0 to 2047, 2048 to 4095, ...) at most 48 rows name the same one
- joint_strain: float32 [2, 128, 6144], P(None, ('gx', 'gy')), may hold values from -4 to 4
- joint_resist: float32 [128, 6144], P(('gx', 'gy')), may hold values from 1 to 2
Outputs:
- warpage: float32 [4096, 4096], P('gx', 'gy')
- strain_next: float32 [2, 128, 6144], P(None, ('gx', 'gy'))
- resist_next: float32 [128, 6144], P(('gx', 'gy'))
Inputs may be any that keep to these rules, and one draw needn't show every extreme that they name: `joint_owner`: among the 2048 joints of one device at most 48 have the same owner, and on some device exactly 48 do.
All inputs are finite; a program needn't handle non-finite values.
Results may differ from a plain program's by a relative error of at most 0.0003.
Values sent between devices are 32-bit elements; how exact they have to be, the bound alone decides.
A program may use at most 320 MiB of HBM per device.

v0:
```python
import jax
import jax.numpy as jnp
from jax import lax
from jax.sharding import PartitionSpec as P

STEPS = 2
SWEEPS = 3


stiffness = 0.2
shear_mod = 0.6
rate_scale = 0.5
sat_level = 2.5
sat_power = 0.3
harden = 2.0


def with_halo(array, sides, width):
    for axis, dim in sides:
        count, length = (lax.axis_size(axis), array.shape[dim])
        up = [(i, (i + 1) % count) for i in range(count - 1)]
        down = [(j, i) for i, j in up]
        last = lax.slice_in_dim(array, length - width, length, axis=dim)
        leading = lax.slice_in_dim(array, 0, width, axis=dim)
        before = lax.ppermute(last, axis, up)
        after = lax.ppermute(leading, axis, down)
        array = jnp.concatenate([before, array, after], axis=dim)
    return array


def thermal_step(ext, heat_rows, lateral, vertical):
    cols = jnp.pad(ext, ((0, 0), (0, 0), (1, 1)))
    center = ext[:, 1:-1]
    lap = ext[:, 2:] + ext[:, :-2] + cols[:, 1:-1, 2:] + cols[:, 1:-1, :-2] - 4.0 * center
    flux = vertical[:, None, None] * (center[1:] - center[:-1])
    vert = jnp.pad(flux, ((0, 1), (0, 0), (0, 0))) - jnp.pad(flux, ((1, 0), (0, 0), (0, 0)))
    return center + lateral[:, None, None] * lap + vert + heat_rows


def moment_of(field, weighting):
    total = weighting[0] * field[0]
    for layer in range(1, field.shape[0]):
        total = total + weighting[layer] * field[layer]
    return total


def sweep(w_pad, e_pad, load):
    center = e_pad[1:-1, 1:-1]
    e_up = 0.5 * (center + e_pad[:-2, 1:-1])
    e_down = 0.5 * (center + e_pad[2:, 1:-1])
    e_left = 0.5 * (center + e_pad[1:-1, :-2])
    e_right = 0.5 * (center + e_pad[1:-1, 2:])
    numer = (
        load
        + e_up * w_pad[:-2, 1:-1]
        + e_down * w_pad[2:, 1:-1]
        + e_left * w_pad[1:-1, :-2]
        + e_right * w_pad[1:-1, 2:]
    )
    denom = stiffness + e_up + e_down + e_left + e_right
    return numer / denom


def anand(strain, resist, recv):
    total, inelastic = (strain[0], strain[1])
    increment, theta, live = (recv[0], recv[1], recv[2])
    total_new = total + increment
    arrhen = jnp.exp(2.0 - 2.0 / (1.0 + 0.1 * theta * theta))
    hyper = jnp.sinh(shear_mod * (total_new - inelastic) / resist)
    rate = rate_scale * arrhen * hyper * jnp.abs(hyper)
    inelastic_new = inelastic + rate
    target = sat_level * jnp.power(1.0 + jnp.abs(rate) / arrhen, sat_power)
    resist_new = resist + harden * (1.0 - resist / target) * jnp.abs(rate)
    keep = live > 0.5
    strain_out = jnp.stack(
        [jnp.where(keep, total_new, total), jnp.where(keep, inelastic_new, inelastic)]
    )
    return (strain_out, jnp.where(keep, resist_new, resist))


def body(
    temp_start,
    heat_input,
    lateral,
    vertical,
    weighting,
    modulus,
    warp_prev,
    joint_cell,
    joint_owner,
    joint_strain,
    joint_resist,
):
    devices = lax.axis_size(("gx", "gy"))
    temp = temp_start
    for step in range(STEPS):
        ext = with_halo(temp, ((("gx", "gy"), 1),), 1)
        temp = thermal_step(ext, heat_input, lateral, vertical)
    relayed = lax.all_to_all(temp, "gy", split_axis=2, concat_axis=1, tiled=True)
    load = moment_of(relayed, weighting)
    top = relayed[-1]
    e_pad = with_halo(modulus, (("gx", 0), ("gy", 1)), 1)
    warp = warp_prev
    for step in range(SWEEPS):
        w_pad = with_halo(warp, (("gx", 0), ("gy", 1)), 1)
        warp = sweep(w_pad, e_pad, load)
    capacity = joint_resist.shape[1] // devices
    owners = joint_owner[:, 0]
    increment = warp.reshape(-1)[joint_cell] - warp_prev.reshape(-1)[joint_cell]
    theta = top.reshape(-1)[joint_cell]
    values = jnp.stack([increment, theta, jnp.ones_like(theta)])
    onehot = (owners[:, None] == jnp.arange(devices, dtype=jnp.int32)[None, :]).astype(jnp.int32)
    ranks = jnp.sum(jnp.cumsum(onehot, axis=0) * onehot, axis=1) - 1
    slots = owners * capacity + ranks
    outgoing = jnp.zeros((3, devices * capacity), jnp.float32).at[:, slots].set(values)
    incoming = lax.all_to_all(outgoing, ("gx", "gy"), split_axis=1, concat_axis=1, tiled=True)
    strain_next, resist_next = anand(joint_strain, joint_resist, incoming[:, None, :])
    return (warp, strain_next, resist_next)


def solution(mesh):
    return jax.shard_map(
        body,
        mesh=mesh,
        in_specs=(
            P(None, ("gx", "gy"), None),
            P(None, ("gx", "gy"), None),
            P(),
            P(),
            P(),
            P("gx", "gy"),
            P("gx", "gy"),
            P(("gx", "gy")),
            P(("gx", "gy"), None),
            P(None, ("gx", "gy"), None),
            P(("gx", "gy"), None),
        ),
        out_specs=(P("gx", "gy"), P(None, ("gx", "gy"), None), P(("gx", "gy"), None)),
        check_vma=False,
    )
```

profile of v0, /device:TPU:1, one launch (start us, length us, event | category | flops | bytes accessed | tf_op | source)
XLA Modules:
  0.0 302.8 jit_solution(859099600028987091)
XLA Ops:
  0.6 4.6 %copy.44 = f32[8,32,4096]{2,0,1:T(8,128)S(1)} copy(f32[8,32,4096]{2,1,0:T(8,128)} %param.11) | data formatting | bytes 8388608 | tf_op args[0]
  5.3 9.5 %collective-permute-start = (f32[8,1,4096]{2,0,1:T(8,128)S(1)}, f32[8,1,4096]{2,0,1:T(8,128)S(1)}, u32[]{:S(2)}, u32[]{:S(2)}) collective-permute-start(f32[8,1,4096]{2,0,1:T(8,128)S(1)} %get-tuple-element.12), channel_id=1, source_target_pairs={{1,0},{2,1},{3,2},{4,3},{5,4},{6,5},{7,6},{8,7},{9,8},{10,9},{11,1... | collective-permute-start | bytes 393224 | tf_op jit(solution)/shard_map/ppermute | solution.py:26
  14.8 1.9 collective-permute-start.1
  16.8 0.7 fusion.8
  17.4 7.4 %collective-permute-done.1 = f32[8,1,4096]{2,0,1:T(8,128)S(1)} collective-permute-done((f32[8,1,4096]{2,0,1:T(8,128)S(1)}, f32[8,1,4096]{2,0,1:T(8,128)S(1)}, u32[]{:S(2)}, u32[]{:S(2)}) %collective-permute-start.1) | collective-permute-done | bytes 131104 | tf_op jit(solution)/shard_map/ppermute | solution.py:25
  24.8 1.3 select_maximum_fusion.2
  26.1 6.8 %fusion.13 = f32[8,32,4096]{2,0,1:T(8,128)S(1)} fusion(f32[8,32,4096]{2,0,1:T(8,128)S(1)} %copy.44, f32[8,34,4098]{2,0,1:T(8,128)S(1)} %select_maximum_fusion.2, f32[8,1,4096]{2,0,1:T(8,128)S(1)} %collective-permute-done.1, f32[8,1,4096]{2,0,1:T(8,128)S(1)} %collective-permute-done, f32[7,32,4096]{2,0,1:T(8,128)S(1)} %fusion.8, f32[8,32,4096]{2,1,0:T(8,128)} %param.12, ...), kind=kLoop, calls=%fused_computation.30 | loop fusion | flops 12582912 | bytes 24903712 | tf_op jit(solution)/shard_map/add | solution.py:37
  33.0 1.9 collective-permute-start.2
  34.9 3.5 %collective-permute-start.3 = (f32[8,1,4096]{2,0,1:T(8,128)S(1)}, f32[8,1,4096]{2,0,1:T(8,128)S(1)}, u32[]{:S(2)}, u32[]{:S(2)}) collective-permute-start(f32[8,1,4096]{2,0,1:T(8,128)S(1)} %get-tuple-element.9), channel_id=1, source_target_pairs={{0,1},{1,2},{2,3},{3,4},{4,5},{5,6},{6,7},{7,8},{8,9},{9,10},{10,1... | collective-permute-start | bytes 393224 | tf_op jit(solution)/shard_map/ppermute | solution.py:25
  38.4 0.7 fusion.1
  39.1 5.7 %collective-permute-done.3 = f32[8,1,4096]{2,0,1:T(8,128)S(1)} collective-permute-done((f32[8,1,4096]{2,0,1:T(8,128)S(1)}, f32[8,1,4096]{2,0,1:T(8,128)S(1)}, u32[]{:S(2)}, u32[]{:S(2)}) %collective-permute-start.3) | collective-permute-done | bytes 131104 | tf_op jit(solution)/shard_map/ppermute | solution.py:25
  44.8 1.3 select_maximum_fusion
  46.1 6.4 %fusion.6 = f32[8,32,4096]{2,0,1:T(8,128)} fusion(f32[8,32,4096]{2,0,1:T(8,128)S(1)} %fusion.13, f32[8,34,4098]{2,0,1:T(8,128)S(1)} %select_maximum_fusion, f32[8,1,4096]{2,0,1:T(8,128)S(1)} %collective-permute-done.3, f32[8,1,4096]{2,0,1:T(8,128)S(1)} %collective-permute-done.2, f32[7,32,4096]{2,0,1:T(8,128)S(1)} %fusion.1, f32[8,32,4096]{2,1,0:T(8,128)S(1)} %copy-done, ...), kind=kLoop, calls=%fused_computation.18 | loop fusion | flops 12582912 | bytes 24903712 | tf_op jit(solution)/shard_map/add | solution.py:37
  52.4 10.8 %copy.49 = f32[8,32,4096]{1,0,2:T(8,128)} copy(f32[8,32,4096]{2,0,1:T(8,128)} %fusion.6) | data formatting | bytes 8388608 | tf_op jit(solution)/shard_map/add | solution.py:37
  63.3 12.8 %reshape.276 = f32[8,1,131072]{2,1,0:T(1,128)} reshape(f32[4096,8,32]{2,1,0:T(8,128)} %bitcast.65) | data formatting | bytes 8388608
  76.1 4.7 %all-to-all-start = ((f32[8,1,131072]{2,1,0:T(1,128)}), f32[8,1,131072]{2,1,0:T(1,128)}, u32[]{:S(2)}, u32[]{:S(2)}) async-start(f32[8,1,131072]{2,1,0:T(1,128)} %reshape.276), calls=%async_computation | async-start | bytes 8388608 | tf_op jit(solution)/shard_map/all_to_all | solution.py:99
  80.8 1.9 collective-permute-start.4
  82.7 2.4 collective-permute-start.6
  85.2 3.2 %collective-permute-start.5 = (f32[1,512]{1,0:T(1,128)S(1)}, f32[1,512]{1,0:T(1,128)S(1)}, u32[]{:S(2)}, u32[]{:S(2)}) collective-permute-start(f32[1,512]{1,0:T(1,128)S(1)} %get-tuple-element.27), channel_id=1, source_target_pairs={{0,8},{8,16},{16,24},{24,32},{32,40},{40,48},{48,56},{56,64},{64,7... | collective-permute-start | bytes 6152 | tf_op jit(solution)/shard_map/ppermute | solution.py:25
  88.4 1.9 collective-permute-start.7
  90.9 0.7 fusion.80
  91.6 1.3 copy.52
  92.9 32.5 %collective-permute-done.4 = f32[1,512]{1,0:T(1,128)S(1)} collective-permute-done((f32[1,512]{1,0:T(1,128)S(1)}, f32[1,512]{1,0:T(1,128)S(1)}, u32[]{:S(2)}, u32[]{:S(2)}) %collective-permute-start.4) | collective-permute-done | bytes 2080 | tf_op jit(solution)/shard_map/ppermute | solution.py:25
  125.4 1.9 collective-permute-done.6
  127.4 1.3 collective-permute-start.10
  128.7 4.1 %collective-permute-start.8 = (f32[258,1]{1,0:T(8,128)S(1)}, f32[258,1]{1,0:T(8,128)S(1)}, u32[]{:S(2)}, u32[]{:S(2)}) collective-permute-start(f32[258,1]{1,0:T(8,128)S(1)} %get-tuple-element.18), channel_id=1, source_target_pairs={{0,1},{1,2},{2,3},{3,4},{4,5},{5,6},{6,7},{8,9},{9,10},{10,11},{11... | collective-permute-start | bytes 3104 | tf_op jit(solution)/shard_map/ppermute | solution.py:25
  133.0 1.3 collective-permute-start.11
  134.3 4.2 %collective-permute-start.9 = (f32[258,1]{1,0:T(8,128)S(1)}, f32[258,1]{1,0:T(8,128)S(1)}, u32[]{:S(2)}, u32[]{:S(2)}) collective-permute-start(f32[258,1]{1,0:T(8,128)S(1)} %get-tuple-element.19), channel_id=1, source_target_pairs={{0,1},{1,2},{2,3},{3,4},{4,5},{5,6},{6,7},{8,9},{9,10},{10,11},{11... | collective-permute-start | bytes 3104 | tf_op jit(solution)/shard_map/ppermute | solution.py:25
  138.5 0.5 broadcast.275
  139.1 13.7 %reduce.13 = f32[8,131072]{1,0:T(8,128)} reduce(f32[8,1,131072]{2,1,0:T(1,128)} %all-to-all-done, f32[]{:T(128)} %broadcast.275), dimensions={1}, to_apply=%all_to_all.17.reduce_sub_computation | reduce | bytes 8388612 | tf_op jit(solution)/shard_map/all_to_all | solution.py:99
  152.7 13.3 %reshape.277 = f32[4096,8,32]{2,1,0:T(8,128)} reshape(f32[8,131072]{1,0:T(8,128)} %reduce.13) | data formatting | bytes 8388608
  166.1 11.4 %copy.50 = f32[8,32,8,512]{3,1,2,0:T(8,128)} copy(f32[8,32,8,512]{1,0,3,2:T(8,128)} %bitcast.66) | data formatting | bytes 8388608 | tf_op jit(solution)/shard_map/all_to_all | solution.py:99
  177.5 7.7 %fusion.73 = (f32[1,8,32,512]{3,2,1,0:T(8,128)S(1)}, f32[1,8,32,512]{3,2,1,0:T(8,128)S(1)}) fusion(f32[8,8,32,512]{3,2,1,0:T(8,128)} %bitcast.67, f32[]{:T(128)} %bitcast.9, f32[]{:T(128)} %bitcast.8, f32[]{:T(128)} %bitcast.7, f32[]{:T(128)} %bitcast.6, f32[]{:T(128)} %bitcast.5, f32[]{:T(128)} %bitcast.4, f32[]{:T(128)} %bitcast.3, f32[]{:T(128)} %bitcast), kind=kLoop, calls=%fused_computation.167 | loop fusion | flops 1966080 | bytes 5242912 | tf_op jit(solution)/shard_map/slice | solution.py:43
  185.3 0.8 fusion.40
  186.1 3.4 %collective-permute-start.12 = (f32[1,512]{1,0:T(1,128)S(1)}, f32[1,512]{1,0:T(1,128)S(1)}, u32[]{:S(2)}, u32[]{:S(2)}) collective-permute-start(f32[1,512]{1,0:T(1,128)S(1)} %get-tuple-element.23), channel_id=1, source_target_pairs={{0,8},{8,16},{16,24},{24,32},{32,40},{40,48},{48,56},{56,64},{64,7... | collective-permute-start | bytes 6152 | tf_op jit(solution)/shard_map/ppermute | solution.py:25
  189.5 1.9 collective-permute-start.13
  191.4 0.6 fusion.17
  192.1 2.4 collective-permute-done.13
  194.5 3.6 %collective-permute-start.14 = (f32[258,1]{1,0:T(8,128)S(1)}, f32[258,1]{1,0:T(8,128)S(1)}, u32[]{:S(2)}, u32[]{:S(2)}) collective-permute-start(f32[258,1]{1,0:T(8,128)S(1)} %get-tuple-element.15), channel_id=1, source_target_pairs={{0,1},{1,2},{2,3},{3,4},{4,5},{5,6},{6,7},{8,9},{9,10},{10,11},{11... | collective-permute-start | bytes 3104 | tf_op jit(solution)/shard_map/ppermute | solution.py:25
  198.1 1.3 collective-permute-start.15
  199.4 0.7 collective-permute-done.14
  200.1 7.4 %collective-permute-done.15 = f32[258,1]{1,0:T(8,128)S(1)} collective-permute-done((f32[258,1]{1,0:T(8,128)S(1)}, f32[258,1]{1,0:T(8,128)S(1)}, u32[]{:S(2)}, u32[]{:S(2)}) %collective-permute-start.15) | collective-permute-done | bytes 1064 | tf_op jit(solution)/shard_map/ppermute | solution.py:26
  207.6 0.8 fusion.31
  208.4 3.2 %collective-permute-start.16 = (f32[1,512]{1,0:T(1,128)S(1)}, f32[1,512]{1,0:T(1,128)S(1)}, u32[]{:S(2)}, u32[]{:S(2)}) collective-permute-start(f32[1,512]{1,0:T(1,128)S(1)} %get-tuple-element.21), channel_id=1, source_target_pairs={{0,8},{8,16},{16,24},{24,32},{32,40},{40,48},{48,56},{56,64},{64,7... | collective-permute-start | bytes 6152 | tf_op jit(solution)/shard_map/ppermute | solution.py:25
  211.6 1.9 collective-permute-start.17
  213.6 0.6 compare_select_fusion.1
  214.2 2.4 collective-permute-done.17
  216.5 0.8 pad_maximum_fusion.38
  217.3 7.2 %collective-permute-start.18 = (f32[258,1]{1,0:T(8,128)}, f32[258,1]{1,0:T(8,128)S(1)}, u32[]{:S(2)}, u32[]{:S(2)}) collective-permute-start(f32[258,1]{1,0:T(8,128)} %get-tuple-element.13), channel_id=1, source_target_pairs={{0,1},{1,2},{2,3},{3,4},{4,5},{5,6},{6,7},{8,9},{9,10},{10,11},{11... | collective-permute-start | bytes 3104 | tf_op jit(solution)/shard_map/ppermute | solution.py:25
  224.6 1.6 collective-permute-start.19
  226.1 0.6 fusion.72
  226.9 12.0 %gather_fusion.1 = f32[2048]{0:T(1024)S(1)} fusion(f32[131072]{0:T(1024)S(1)} %bitcast.64, s32[2048]{0:T(1024)} %fusion.72), kind=kCustom, calls=%fused_computation.1 | custom fusion | bytes 24576 | tf_op jit(solution)/shard_map/gather | solution.py:109
  239.1 11.8 %gather_fusion.2 = f32[2048]{0:T(1024)S(1)} fusion(f32[131072]{0:T(1024)S(1)} %bitcast.62, s32[2048]{0:T(1024)S(1)} %copy-done.6), kind=kCustom, calls=%fused_computation.2 | custom fusion | bytes 24576 | tf_op jit(solution)/shard_map/gather | solution.py:110
  251.0 1.7 fusion.22
  252.6 0.8 copy-done.4
  253.6 11.8 %gather_fusion = f32[2048]{0:T(1024)S(1)} fusion(f32[131072]{0:T(1024)S(1)} %bitcast.63, s32[2048]{0:T(1024)S(1)} %copy-done.6), kind=kCustom, calls=%fused_computation | custom fusion | bytes 24576 | tf_op jit(solution)/shard_map/gather | solution.py:109
  265.4 1.4 copy.53
  266.8 6.7 %scatter_custom_fusion = f32[3,6144]{0,1:T(8,128)S(1)} fusion(s32[2048]{0:T(1024)} %bitcast.81, f32[2048,3]{1,0:T(8,128)} %copy.53, f32[]{:T(128)} %constant.16.clone.1), kind=kCustom, calls=%fused_computation.35 | custom fusion | bytes 74240 | tf_op jit(solution)/shard_map/scatter | solution.py:115
  273.5 1.4 copy.54
  275.2 23.3 %all_to_all.24 = f32[128,1,144]{2,1,0:T(1,128)S(1)} all-to-all(f32[128,1,144]{2,1,0:T(1,128)S(1)} %reshape.278), channel_id=1, replica_groups=mesh['gx'=16,'gy'=8] {'gx','gy'}, dimensions={0} | all-to-all | bytes 147456 | tf_op jit(solution)/shard_map/all_to_all | solution.py:116
  298.5 0.9 reduce.14
  299.6 0.4 slice_reduce_fusion.1
  300.9 1.1 add_select_fusion
  302.1 0.7 pad_maximum_fusion.48
  (82 shorter events, 2.9 us)
Async XLA Ops:
  0.6 16.1 %copy-start.17 = (f32[7]{0:T(128)S(1)}, f32[7]{0:T(128)}, u32[]{:S(2)}) copy-start(f32[7]{0:T(128)} %param.14) | copy-start | bytes 88
  5.3 12.1 %collective-permute-start = (f32[8,1,4096]{2,0,1:T(8,128)S(1)}, f32[8,1,4096]{2,0,1:T(8,128)S(1)}, u32[]{:S(2)}, u32[]{:S(2)}) collective-permute-start(f32[8,1,4096]{2,0,1:T(8,128)S(1)} %get-tuple-element.12), channel_id=1, source_target_pairs={{1,0},{2,1},{3,2},{4,3},{5,4},{6,5},{7,6},{8,7},{9,8},{10,9},{11,1... | collective-permute-start | bytes 393224 | tf_op jit(solution)/shard_map/ppermute | solution.py:26
  14.8 10.0 %collective-permute-start.1 = (f32[8,1,4096]{2,0,1:T(8,128)S(1)}, f32[8,1,4096]{2,0,1:T(8,128)S(1)}, u32[]{:S(2)}, u32[]{:S(2)}) collective-permute-start(f32[8,1,4096]{2,0,1:T(8,128)S(1)} %get-tuple-element.11), channel_id=1, source_target_pairs={{0,1},{1,2},{2,3},{3,4},{4,5},{5,6},{6,7},{7,8},{8,9},{9,10},{10,1... | collective-permute-start | bytes 393224 | tf_op jit(solution)/shard_map/ppermute | solution.py:25
  17.4 8.7 %copy-start.18 = (f32[8]{0:T(128)S(1)}, f32[8]{0:T(128)}, u32[]{:S(2)}) copy-start(f32[8]{0:T(128)} %param.13) | copy-start | bytes 100
  33.0 6.2 %collective-permute-start.2 = (f32[8,1,4096]{2,0,1:T(8,128)S(1)}, f32[8,1,4096]{2,0,1:T(8,128)S(1)}, u32[]{:S(2)}, u32[]{:S(2)}) collective-permute-start(f32[8,1,4096]{2,0,1:T(8,128)S(1)} %get-tuple-element.10), channel_id=1, source_target_pairs={{1,0},{2,1},{3,2},{4,3},{5,4},{6,5},{7,6},{8,7},{9,8},{10,9},{11,1... | collective-permute-start | bytes 393224 | tf_op jit(solution)/shard_map/ppermute | solution.py:26
  34.9 9.9 %collective-permute-start.3 = (f32[8,1,4096]{2,0,1:T(8,128)S(1)}, f32[8,1,4096]{2,0,1:T(8,128)S(1)}, u32[]{:S(2)}, u32[]{:S(2)}) collective-permute-start(f32[8,1,4096]{2,0,1:T(8,128)S(1)} %get-tuple-element.9), channel_id=1, source_target_pairs={{0,1},{1,2},{2,3},{3,4},{4,5},{5,6},{6,7},{7,8},{8,9},{9,10},{10,1... | collective-permute-start | bytes 393224 | tf_op jit(solution)/shard_map/ppermute | solution.py:25
  39.1 6.9 %copy-start = (f32[8,32,4096]{2,1,0:T(8,128)S(1)}, f32[8,32,4096]{2,1,0:T(8,128)}, u32[]{:S(2)}) copy-start(f32[8,32,4096]{2,1,0:T(8,128)} %param.12) | copy-start | bytes 12582916
  76.1 4.7 %copy-start.1 = (f32[256,512]{1,0:T(8,128)S(1)}, f32[256,512]{1,0:T(8,128)}, u32[]{:S(2)}) copy-start(f32[256,512]{1,0:T(8,128)} %param.16) | copy-start | bytes 1572868
  76.1 9.1 %copy-start.2 = (f32[256,512]{1,0:T(8,128)S(1)}, f32[256,512]{1,0:T(8,128)}, u32[]{:S(2)}) copy-start(f32[256,512]{1,0:T(8,128)} %param.17) | copy-start | bytes 1572868
  76.1 14.2 %copy-start.7 = (s32[2048,1]{0,1:T(1,128)S(1)}, s32[2048,1]{0,1:T(1,128)}, u32[]{:S(2)}) copy-start(s32[2048,1]{0,1:T(1,128)} %param.19) | copy-start | bytes 24580
  76.1 14.8 %copy-start.10 = (f32[8]{0:T(128)S(1)}, f32[8]{0:T(128)}, u32[]{:S(2)}) copy-start(f32[8]{0:T(128)} %param.15) | copy-start | bytes 100
  76.1 62.5 %all-to-all-start = ((f32[8,1,131072]{2,1,0:T(1,128)}), f32[8,1,131072]{2,1,0:T(1,128)}, u32[]{:S(2)}, u32[]{:S(2)}) async-start(f32[8,1,131072]{2,1,0:T(1,128)} %reshape.276), calls=%async_computation | async-start | bytes 8388608 | tf_op jit(solution)/shard_map/all_to_all | solution.py:99
  80.8 44.6 %collective-permute-start.4 = (f32[1,512]{1,0:T(1,128)S(1)}, f32[1,512]{1,0:T(1,128)S(1)}, u32[]{:S(2)}, u32[]{:S(2)}) collective-permute-start(f32[1,512]{1,0:T(1,128)S(1)} %get-tuple-element.26), channel_id=1, source_target_pairs={{0,8},{8,16},{16,24},{24,32},{32,40},{40,48},{48,56},{56,64},{64,7... | collective-permute-start | bytes 6152 | tf_op jit(solution)/shard_map/ppermute | solution.py:25
  82.7 44.6 %collective-permute-start.6 = (f32[1,512]{1,0:T(1,128)S(1)}, f32[1,512]{1,0:T(1,128)S(1)}, u32[]{:S(2)}, u32[]{:S(2)}) collective-permute-start(f32[1,512]{1,0:T(1,128)S(1)} %get-tuple-element.25), channel_id=1, source_target_pairs={{8,0},{16,8},{24,16},{32,24},{40,32},{48,40},{56,48},{64,56},{72,6... | collective-permute-start | bytes 6152 | tf_op jit(solution)/shard_map/ppermute | solution.py:26
  85.2 47.7 %collective-permute-start.5 = (f32[1,512]{1,0:T(1,128)S(1)}, f32[1,512]{1,0:T(1,128)S(1)}, u32[]{:S(2)}, u32[]{:S(2)}) collective-permute-start(f32[1,512]{1,0:T(1,128)S(1)} %get-tuple-element.27), channel_id=1, source_target_pairs={{0,8},{8,16},{16,24},{24,32},{32,40},{40,48},{48,56},{56,64},{64,7... | collective-permute-start | bytes 6152 | tf_op jit(solution)/shard_map/ppermute | solution.py:25
  88.4 44.5 %collective-permute-start.7 = (f32[1,512]{1,0:T(1,128)S(1)}, f32[1,512]{1,0:T(1,128)S(1)}, u32[]{:S(2)}, u32[]{:S(2)}) collective-permute-start(f32[1,512]{1,0:T(1,128)S(1)} %get-tuple-element.28), channel_id=1, source_target_pairs={{8,0},{16,8},{24,16},{32,24},{40,32},{48,40},{56,48},{64,56},{72,6... | collective-permute-start | bytes 6152 | tf_op jit(solution)/shard_map/ppermute | solution.py:26
  127.3 80.2 %copy-start.8 = (f32[1,512]{1,0:T(1,128)}, f32[1,512]{1,0:T(1,128)S(1)}, u32[]{:S(2)}) copy-start(f32[1,512]{1,0:T(1,128)S(1)} %collective-permute-done.6) | copy-start | bytes 6148
  127.4 57.8 %collective-permute-start.10 = (f32[258,1]{1,0:T(8,128)S(1)}, f32[258,1]{1,0:T(8,128)S(1)}, u32[]{:S(2)}, u32[]{:S(2)}) collective-permute-start(f32[258,1]{1,0:T(8,128)S(1)} %get-tuple-element.17), channel_id=1, source_target_pairs={{1,0},{2,1},{3,2},{4,3},{5,4},{6,5},{7,6},{9,8},{10,9},{11,10},{12... | collective-permute-start | bytes 3104 | tf_op jit(solution)/shard_map/ppermute | solution.py:26
  128.7 56.5 %collective-permute-start.8 = (f32[258,1]{1,0:T(8,128)S(1)}, f32[258,1]{1,0:T(8,128)S(1)}, u32[]{:S(2)}, u32[]{:S(2)}) collective-permute-start(f32[258,1]{1,0:T(8,128)S(1)} %get-tuple-element.18), channel_id=1, source_target_pairs={{0,1},{1,2},{2,3},{3,4},{4,5},{5,6},{6,7},{8,9},{9,10},{10,11},{11... | collective-permute-start | bytes 3104 | tf_op jit(solution)/shard_map/ppermute | solution.py:25
  133.0 52.3 %collective-permute-start.11 = (f32[258,1]{1,0:T(8,128)S(1)}, f32[258,1]{1,0:T(8,128)S(1)}, u32[]{:S(2)}, u32[]{:S(2)}) collective-permute-start(f32[258,1]{1,0:T(8,128)S(1)} %get-tuple-element.20), channel_id=1, source_target_pairs={{1,0},{2,1},{3,2},{4,3},{5,4},{6,5},{7,6},{9,8},{10,9},{11,10},{12... | collective-permute-start | bytes 3104 | tf_op jit(solution)/shard_map/ppermute | solution.py:26
  134.3 51.0 %collective-permute-start.9 = (f32[258,1]{1,0:T(8,128)S(1)}, f32[258,1]{1,0:T(8,128)S(1)}, u32[]{:S(2)}, u32[]{:S(2)}) collective-permute-start(f32[258,1]{1,0:T(8,128)S(1)} %get-tuple-element.19), channel_id=1, source_target_pairs={{0,1},{1,2},{2,3},{3,4},{4,5},{5,6},{6,7},{8,9},{9,10},{10,11},{11... | collective-permute-start | bytes 3104 | tf_op jit(solution)/shard_map/ppermute | solution.py:25
  177.5 13.9 %copy-start.3 = (s32[128,16,128]{0,2,1:T(8,128)S(1)}, s32[128,16,128]{0,2,1:T(8,128)}, u32[]{:S(2)}) copy-start(s32[128,16,128]{0,2,1:T(8,128)} %copy.52) | copy-start | bytes 3145732
  185.2 40.9 %copy-start.16 = (s32[2048]{0:T(1024)S(1)}, s32[2048]{0:T(1024)}, u32[]{:S(2)}) copy-start(s32[2048]{0:T(1024)} %param.18) | copy-start | bytes 24580
  186.1 6.0 %collective-permute-start.12 = (f32[1,512]{1,0:T(1,128)S(1)}, f32[1,512]{1,0:T(1,128)S(1)}, u32[]{:S(2)}, u32[]{:S(2)}) collective-permute-start(f32[1,512]{1,0:T(1,128)S(1)} %get-tuple-element.23), channel_id=1, source_target_pairs={{0,8},{8,16},{16,24},{24,32},{32,40},{40,48},{48,56},{56,64},{64,7... | collective-permute-start | bytes 6152 | tf_op jit(solution)/shard_map/ppermute | solution.py:25
  189.5 4.9 %collective-permute-start.13 = (f32[1,512]{1,0:T(1,128)S(1)}, f32[1,512]{1,0:T(1,128)S(1)}, u32[]{:S(2)}, u32[]{:S(2)}) collective-permute-start(f32[1,512]{1,0:T(1,128)S(1)} %get-tuple-element.24), channel_id=1, source_target_pairs={{8,0},{16,8},{24,16},{32,24},{40,32},{48,40},{56,48},{64,56},{72,6... | collective-permute-start | bytes 6152 | tf_op jit(solution)/shard_map/ppermute | solution.py:26
  194.5 5.6 %collective-permute-start.14 = (f32[258,1]{1,0:T(8,128)S(1)}, f32[258,1]{1,0:T(8,128)S(1)}, u32[]{:S(2)}, u32[]{:S(2)}) collective-permute-start(f32[258,1]{1,0:T(8,128)S(1)} %get-tuple-element.15), channel_id=1, source_target_pairs={{0,1},{1,2},{2,3},{3,4},{4,5},{5,6},{6,7},{8,9},{9,10},{10,11},{11... | collective-permute-start | bytes 3104 | tf_op jit(solution)/shard_map/ppermute | solution.py:25
  198.1 9.4 %collective-permute-start.15 = (f32[258,1]{1,0:T(8,128)S(1)}, f32[258,1]{1,0:T(8,128)S(1)}, u32[]{:S(2)}, u32[]{:S(2)}) collective-permute-start(f32[258,1]{1,0:T(8,128)S(1)} %get-tuple-element.16), channel_id=1, source_target_pairs={{1,0},{2,1},{3,2},{4,3},{5,4},{6,5},{7,6},{9,8},{10,9},{11,10},{12... | collective-permute-start | bytes 3104 | tf_op jit(solution)/shard_map/ppermute | solution.py:26
  208.4 5.8 %collective-permute-start.16 = (f32[1,512]{1,0:T(1,128)S(1)}, f32[1,512]{1,0:T(1,128)S(1)}, u32[]{:S(2)}, u32[]{:S(2)}) collective-permute-start(f32[1,512]{1,0:T(1,128)S(1)} %get-tuple-element.21), channel_id=1, source_target_pairs={{0,8},{8,16},{16,24},{24,32},{32,40},{40,48},{48,56},{56,64},{64,7... | collective-permute-start | bytes 6152 | tf_op jit(solution)/shard_map/ppermute | solution.py:25
  211.6 4.9 %collective-permute-start.17 = (f32[1,512]{1,0:T(1,128)S(1)}, f32[1,512]{1,0:T(1,128)S(1)}, u32[]{:S(2)}, u32[]{:S(2)}) collective-permute-start(f32[1,512]{1,0:T(1,128)S(1)} %get-tuple-element.22), channel_id=1, source_target_pairs={{8,0},{16,8},{24,16},{32,24},{40,32},{48,40},{56,48},{64,56},{72,6... | collective-permute-start | bytes 6152 | tf_op jit(solution)/shard_map/ppermute | solution.py:26
  214.2 12.6 %copy-start.12 = (f32[1,512]{1,0:T(1,128)}, f32[1,512]{1,0:T(1,128)S(1)}, u32[]{:S(2)}) copy-start(f32[1,512]{1,0:T(1,128)S(1)} %collective-permute-done.16) | copy-start | bytes 6148
  216.5 10.2 %copy-start.14 = (f32[1,512]{1,0:T(1,128)}, f32[1,512]{1,0:T(1,128)S(1)}, u32[]{:S(2)}) copy-start(f32[1,512]{1,0:T(1,128)S(1)} %collective-permute-done.17) | copy-start | bytes 6148
  217.3 33.6 %collective-permute-start.18 = (f32[258,1]{1,0:T(8,128)}, f32[258,1]{1,0:T(8,128)S(1)}, u32[]{:S(2)}, u32[]{:S(2)}) collective-permute-start(f32[258,1]{1,0:T(8,128)} %get-tuple-element.13), channel_id=1, source_target_pairs={{0,1},{1,2},{2,3},{3,4},{4,5},{5,6},{6,7},{8,9},{9,10},{10,11},{11... | collective-permute-start | bytes 3104 | tf_op jit(solution)/shard_map/ppermute | solution.py:25
  224.6 26.4 %collective-permute-start.19 = (f32[258,1]{1,0:T(8,128)}, f32[258,1]{1,0:T(8,128)}, u32[]{:S(2)}, u32[]{:S(2)}) collective-permute-start(f32[258,1]{1,0:T(8,128)} %get-tuple-element.14), channel_id=1, source_target_pairs={{1,0},{2,1},{3,2},{4,3},{5,4},{6,5},{7,6},{9,8},{10,9},{11,10},{12... | collective-permute-start | bytes 3104 | tf_op jit(solution)/shard_map/ppermute | solution.py:26
  226.9 12.2 %copy-start.6 = (s32[2048]{0:T(1024)S(1)}, s32[2048]{0:T(1024)}, u32[]{:S(2)}) copy-start(s32[2048]{0:T(1024)} %fusion.72) | copy-start | bytes 24580
  239.1 11.8 %copy-start.9 = (f32[1,512]{1,0:T(1,128)S(1)}, f32[1,512]{1,0:T(1,128)}, u32[]{:S(2)}) copy-start(f32[1,512]{1,0:T(1,128)} %copy-done.8) | copy-start | bytes 6148
  239.1 11.8 %copy-start.13 = (f32[1,512]{1,0:T(1,128)S(1)}, f32[1,512]{1,0:T(1,128)}, u32[]{:S(2)}) copy-start(f32[1,512]{1,0:T(1,128)} %copy-done.12) | copy-start | bytes 6148
  239.1 11.8 %copy-start.15 = (f32[1,512]{1,0:T(1,128)S(1)}, f32[1,512]{1,0:T(1,128)}, u32[]{:S(2)}) copy-start(f32[1,512]{1,0:T(1,128)} %copy-done.14) | copy-start | bytes 6148
  252.6 0.8 copy-start.4
  266.8 34.1 %copy-start.5 = (f32[2,1,6144]{2,1,0:T(1,128)S(1)}, f32[2,1,6144]{2,1,0:T(1,128)}, u32[]{:S(2)}) copy-start(f32[2,1,6144]{2,1,0:T(1,128)} %param.20) | copy-start | bytes 147460
  266.8 34.1 %copy-start.11 = (f32[1,6144]{1,0:T(1,128)S(1)}, f32[1,6144]{1,0:T(1,128)}, u32[]{:S(2)}) copy-start(f32[1,6144]{1,0:T(1,128)} %param.21) | copy-start | bytes 73732
where the time goes:
time: 304 us; the launch traced here: 303 us
  local copies, waits for them, and re-layouts  103 us (34%)
  starting transfers between devices  66.1 us (22%)
  waiting for transfers between devices  60.3 us (20%)
  other arithmetic  48.2 us (16%)
  blocking collectives  23.3 us (8%)
    ppermute x10, waiting for transfers between devices, with_halo(): before = lax.ppermute(last, axis, up)  46.3 us
    ppermute x10, starting transfers between devices, with_halo(): before = lax.ppermute(last, axis, up)  36.3 us
    unnamed x46, local copies, waits for them, and re-layouts  32.5 us
    ppermute x10, starting transfers between devices, with_halo(): after = lax.ppermute(leading, axis, down)  25 us
    gather x2, local copies, waits for them, and re-layouts, body(): increment = warp.reshape(-1)[joint_cell] - warp_prev.reshape(-1)[joint_cell]  23.7 us
    all_to_all x1, blocking collectives, body(): lax.all_to_all(outgoing, ('gx', 'gy'), split_axis=1, concat_axis=1, tiled...  23.3 us
    ppermute x10, waiting for transfers between devices, with_halo(): after = lax.ppermute(leading, axis, down)  14.1 us
    all_to_all x1, other arithmetic, body(): lax.all_to_all(temp, 'gy', split_axis=2, concat_axis=1, tiled=True)  13.7 us
  transfers between devices with their start and end apart: 21, of which 8 were waited for; matrix products, arithmetic and copies ran while one was open for 25% of the time, Pallas kernels for 0%

commit v1 on v0

v1 whole, which is shorter than its diff:
```python
import functools

import jax
import jax.numpy as jnp
from jax import lax
from jax.experimental import pallas as pl
from jax.experimental.pallas import tpu as pltpu
from jax.sharding import PartitionSpec as P

MESH = pl.DeviceIdType.MESH
F32 = jnp.float32
BF16 = jnp.bfloat16

stiffness = 0.2
shear_mod = 0.6
rate_scale = 0.5
sat_level = 2.5
sat_power = 0.3
harden = 2.0
LN2 = 0.6931471805599453


def iota(shape, dim):
    return lax.broadcasted_iota(jnp.int32, shape, dim)


def split(x):
    hi = x.astype(BF16)
    return hi, (x - hi.astype(F32)).astype(BF16)


def layer_weights(lat, ver, w):
    n = len(w)

    def add(x, y):
        return y if x is None else x if y is None else x + y

    def mul(x, y):
        return None if x is None else x * y

    def vert(x):
        out = []
        for l in range(n):
            keep = 1.0
            if l < n - 1:
                keep = keep - ver[l]
            if l > 0:
                keep = keep - ver[l - 1]
            total = mul(x[l], keep)
            if l > 0:
                total = add(total, mul(x[l - 1], ver[l - 1]))
            if l < n - 1:
                total = add(total, mul(x[l + 1], ver[l]))
            out.append(total)
        return out

    u = vert(w)
    wd = [mul(x, d) for x, d in zip(w, lat)]
    a0 = vert(u)
    a1 = [add(mul(x, d), y) for x, d, y in zip(u, lat, vert(wd))]
    a2 = [mul(x, d) for x, d in zip(wd, lat)]
    b0 = [add(x, y) for x, y in zip(u, w)]
    return (a0, b0), (a1, wd), (a2, [None] * n)


def kernel(
    n_gx,
    n_gy,
    temp_ref,
    heat_ref,
    lat_ref,
    ver_ref,
    wei_ref,
    mod_ref,
    prev_ref,
    cell_ref,
    owner_ref,
    strain_ref,
    resist_ref,
    warp_out,
    strain_out,
    resist_out,
    tbuf,
    hbuf,
    sums,
    msg_s,
    msg_r,
    cross_s,
    cross_r,
    col_s,
    col_r,
    row_s,
    row_r,
    mw,
    wbuf,
    coef,
    load,
    edges,
    top,
    oh_row,
    oh_own,
    slot_of,
    ft_hi,
    ft_lo,
    inc_of,
    theta_of,
    out1_s,
    out1_r,
    out2_s,
    out2_r,
    load_sem,
    aux_sem,
    out_sem,
    col_ss,
    col_rs,
    row_ss,
    row_rs,
    msg_ss,
    msg_rs,
    cross_ss,
    cross_rs,
    one_ss,
    one_rs,
    two_ss,
    two_rs,
):
    layers, tr, columns = temp_ref.shape
    rm, cm = mod_ref.shape
    blocks = tr // 8
    nrow = rm + 8
    ext = cm + 128
    cj = cm // 128
    devices = n_gx * n_gy
    cap = resist_ref.shape[0] * 128 // devices
    jpd = cell_ref.shape[1]
    mwide = blocks * cm + cm // 2 + 128
    twide = blocks * cm + cm // 2
    gx, gy = lax.axis_index("gx"), lax.axis_index("gy")
    last_x, last_y = n_gx - 1, n_gy - 1

    def chunk_of(k):
        return lax.rem(gy + k, n_gy)

    def chunk_copies(k):
        cols = pl.ds(pl.multiple_of(chunk_of(k) * cm, cm), cm)
        return (
            pltpu.make_async_copy(temp_ref.at[:, :, cols], tbuf.at[k], load_sem.at[0, k]),
            pltpu.make_async_copy(heat_ref.at[:, :, cols], hbuf.at[k], load_sem.at[1, k]),
        )

    def mw_copies():
        return [
            pltpu.make_async_copy(
                ref, mw.at[i, pl.ds(0, rm), pl.ds(0, cm)], aux_sem.at[i]
            )
            for i, ref in enumerate((mod_ref, prev_ref))
        ]

    for copy in mw_copies():
        copy.start()

    @pl.loop(0, n_gy)
    def _(k):
        for copy in chunk_copies(k):
            copy.start()

    @pl.when(gy == last_y)
    def _():
        col_r[0] = jnp.zeros_like(col_r[0])

    @pl.when(gy == 0)
    def _():
        col_r[1] = jnp.zeros_like(col_r[1])

    @pl.when(gx == last_x)
    def _():
        row_r[0] = jnp.zeros_like(row_r[0])
        cross_r[0] = jnp.zeros_like(cross_r[0])

    @pl.when(gx == 0)
    def _():
        row_r[1] = jnp.zeros_like(row_r[1])
        cross_r[1] = jnp.zeros_like(cross_r[1])

    barrier = pltpu.get_barrier_semaphore()

    @pl.loop(1, n_gy)
    def _(d):
        pl.semaphore_signal(
            barrier, inc=1, device_id=(gx, lax.rem(gy + d, n_gy)), device_id_type=MESH
        )

    @pl.loop(1, n_gx)
    def _(d):
        pl.semaphore_signal(
            barrier, inc=1, device_id=(lax.rem(gx + d, n_gx), gy), device_id_type=MESH
        )

    @pl.when(gx < last_x)
    def _():
        pl.semaphore_signal(barrier, inc=1, device_id=(gx + 1, 0), device_id_type=MESH)

    @pl.when(gx > 0)
    def _():
        pl.semaphore_signal(
            barrier, inc=1, device_id=(gx - 1, last_y), device_id_type=MESH
        )

    lat = [lat_ref[i] for i in range(layers)]
    ver = [ver_ref[i] for i in range(layers - 1)]
    wei = [wei_ref[i] for i in range(layers)]
    fields = [
        layer_weights(lat, ver, wei),
        layer_weights(lat, ver, [None] * (layers - 1) + [1.0]),
    ]

    zero_cols = jnp.zeros((tr, 128), F32)
    for f in range(2):
        for p in range(3):
            sums[f, p, :, 0:128] = zero_cols
            sums[f, p, :, columns + 128 : columns + 256] = zero_cols

    lane8 = iota((8, 128), 1)
    for copy in mw_copies():
        copy.wait()
    for i in range(2):
        to_left = jnp.zeros((8, 128), F32)
        to_right = jnp.zeros((8, 128), F32)
        for b in range(rm // 8):
            here = (lane8 >= 4 * b) & (lane8 < 4 * b + 4)
            lo = mw[i, 8 * b : 8 * b + 8, 0:128]
            hi = mw[i, 8 * b : 8 * b + 8, cm - 128 : cm]
            to_left = jnp.where(here, pltpu.roll(lo, 4 * b, 1), to_left)
            to_right = jnp.where(here, pltpu.roll(hi, (4 * b + 4) % 128, 1), to_right)
        col_s[0, i] = to_left
        col_s[1, i] = to_right

    greeted = n_gy - 1 + n_gx - 1
    more_up = jnp.where((gy == 0) & (gx > 0), n_gy, 0)
    more_down = jnp.where((gy == last_y) & (gx < last_x), n_gy, 0)
    pl.semaphore_wait(barrier, greeted + more_up + more_down)

    def col_copy(side, to):
        return pltpu.make_async_remote_copy(
            src_ref=col_s.at[side],
            dst_ref=col_r.at[side],
            send_sem=col_ss.at[side],
            recv_sem=col_rs.at[side],
            device_id=(gx, to),
            device_id_type=MESH,
        )

    def row_copy(side, to):
        return pltpu.make_async_remote_copy(
            src_ref=row_s.at[side],
            dst_ref=row_r.at[side],
            send_sem=row_ss.at[side],
            recv_sem=row_rs.at[side],
            device_id=(to, gy),
            device_id_type=MESH,
        )

    @pl.when(gy > 0)
    def _():
        col_copy(0, gy - 1).start()

    @pl.when(gy < last_y)
    def _():
        col_copy(1, gy + 1).start()

    def layer_sums(k):
        for copy in chunk_copies(k):
            copy.wait()
        base = 128 + chunk_of(k) * cm
        for j in range(cj):
            lanes = slice(j * 128, j * 128 + 128)
            acc = [[None] * 3, [None] * 3]
            for l in range(layers):
                t, h = tbuf[k, l, :, lanes], hbuf[k, l, :, lanes]
                for f in range(2):
                    for p in range(3):
                        a, b = fields[f][p]
                        for c, x in ((a[l], t), (b[l], h)):
                            if c is not None:
                                term = c * x
                                acc[f][p] = (
                                    term if acc[f][p] is None else acc[f][p] + term
                                )
            where = pl.ds(pl.multiple_of(base + j * 128, 128), 128)
            for f in range(2):
                for p in range(3):
                    sums[f, p, :, where] = acc[f][p]

    wide = cm + 256
    crow = tr + 8

    def neighbours(x):
        r, c = x.shape
        return (
            pltpu.roll(x, 1, 0)
            + pltpu.roll(x, r - 1, 0)
            + pltpu.roll(x, 1, 1)
            + pltpu.roll(x, c - 1, 1)
            - 4.0 * x
        )

    sub8 = iota((8, cm // 2), 0)

    def contribution(f, c):
        window = pl.ds(pl.multiple_of(c * cm, cm), wide)
        zero = jnp.zeros((8, wide), F32)
        p0, p1, p2 = (
            jnp.concatenate([sums[f, p, :, window], zero], axis=0) for p in range(3)
        )
        q = p1 + neighbours(p2)
        col = c * cm - 128 + iota((crow, wide), 1)
        row = iota((crow, wide), 0)
        panel = (col >= 0) & (col < columns)
        panel = panel & ((row < tr + 4) | (gx > 0) | (gy > 0))
        panel = panel & (
            (row < tr) | (row >= tr + 4) | (gx < last_x) | (gy < last_y)
        )
        q = jnp.where(panel, q, 0.0)
        out = p0 + neighbours(q)
        main = out[:, 128 : 128 + cm]
        lane = iota((crow, 128), 1)
        halo = jnp.where(lane < 64, out[:, 128 + cm :], out[:, 0:128])
        return main, halo

    def write_message(ref, main, halo):
        for b in range(blocks):
            ref[:, b * cm : b * cm + cm] = main[8 * b : 8 * b + 8]
        edge = main[tr:]
        half = cm // 2
        at = blocks * cm
        ref[:, at : at + half] = jnp.where(
            (sub8 < 2) | (sub8 >= 6), edge[:, :half], pltpu.roll(edge[:, half:], 4, 0)
        )
        if halo is not None:
            packed = halo[0:8]
            for b in range(1, blocks + 1):
                here = (lane8 >= 8 * b - 2) & (lane8 < 8 * b + 2)
                packed = jnp.where(
                    here, pltpu.roll(halo[8 * b : 8 * b + 8], 8 * b, 1), packed
                )
            ref[:, at + half : at + half + 128] = packed

    def msg_copy(f, k):
        cols = pl.ds(0, mwide if f == 0 else twide)
        return pltpu.make_async_remote_copy(
            src_ref=msg_s.at[f, k, :, cols],
            dst_ref=msg_r.at[f, gy, :, cols],
            send_sem=msg_ss.at[f, k],
            recv_sem=msg_rs.at[f, gy],
            device_id=(gx, chunk_of(k)),
            device_id_type=MESH,
        )

    def msg_arrival(f, s):
        cols = pl.ds(0, mwide if f == 0 else twide)
        return pltpu.make_async_remote_copy(
            src_ref=msg_s.at[f, 0, :, cols],
            dst_ref=msg_r.at[f, s, :, cols],
            send_sem=msg_ss.at[f, 0],
            recv_sem=msg_rs.at[f, s],
            device_id=(gx, s),
            device_id_type=MESH,
        )

    def cross_copy(side, f, k):
        return pltpu.make_async_remote_copy(
            src_ref=cross_s.at[f, k],
            dst_ref=cross_r.at[side, f],
            send_sem=cross_ss.at[f, k],
            recv_sem=cross_rs.at[side, f],
            device_id=(gx - 1 if side == 0 else gx + 1, chunk_of(k)),
            device_id_type=MESH,
        )

    sends_up = (gy == 0) & (gx > 0)
    sends_down = (gy == last_y) & (gx < last_x)
    sub_e = iota((8, ext), 0)

    def finish(f, k, own):
        main, halo = contribution(f, chunk_of(k))

        @pl.when(sends_up)
        def _():
            block = jnp.concatenate([main, halo], axis=1)
            cross_s[f, k] = jnp.where(sub_e < 4, block[0:8], block[tr:])
            cross_copy(0, f, k).start()

        @pl.when(sends_down)
        def _():
            block = jnp.concatenate([main, halo], axis=1)
            cross_s[f, k] = jnp.where(sub_e >= 4, block[tr - 8 : tr], block[tr:])
            cross_copy(1, f, k).start()

        if own:
            write_message(msg_r.at[f, gy], main, halo if f == 0 else None)
        else:
            write_message(msg_s.at[f, k], main, halo if f == 0 else None)
            msg_copy(f, k).start()

    layer_sums(0)
    layer_sums(1)

    @pl.loop(2, n_gy + 1)
    def _(k):
        @pl.when(k < n_gy)
        def _():
            layer_sums(k)

        finish(0, k - 1, False)

    finish(0, 0, True)

    @pl.when(gy < last_y)
    def _():
        col_copy(0, gy).wait_recv()

    @pl.when(gy > 0)
    def _():
        col_copy(1, gy).wait_recv()

    for i in range(2):
        right, left = col_r[0, i], col_r[1, i]
        for b in range(rm // 8):
            mw[i, 8 * b : 8 * b + 8, cm:ext] = jnp.where(
                lane8 < 64,
                pltpu.roll(right, (128 - 4 * b) % 128, 1),
                pltpu.roll(left, (256 - 4 * b - 4) % 128, 1),
            )
        row_s[0, i] = mw[i, 0:8, :]
        row_s[1, i] = mw[i, rm - 8 : rm, :]

    @pl.when(gx > 0)
    def _():
        row_copy(0, gx - 1).start()

    @pl.when(gx < last_x)
    def _():
        row_copy(1, gx + 1).start()

    @pl.loop(1, n_gy)
    def _(k):
        finish(1, k, False)

    finish(1, 0, True)

    aux = (
        pltpu.make_async_copy(cell_ref, inc_of.at[0], aux_sem.at[2]),
        pltpu.make_async_copy(owner_ref, inc_of.at[1], aux_sem.at[3]),
    )
    for copy in aux:
        copy.start()
    state = (
        pltpu.make_async_copy(strain_ref, strain_out, aux_sem.at[4]),
        pltpu.make_async_copy(resist_ref, resist_out, aux_sem.at[5]),
    )
    for copy in state:
        copy.start()
    for copy in aux:
        copy.wait()
    jb = 256
    upper = (iota((jb, jb), 0) < iota((jb, jb), 1)).astype(F32).astype(BF16)
    own_rows = iota((devices, jb), 0)
    cell_rows = iota((rm, jb), 0)
    carry = jnp.zeros((devices, 1), F32)
    shift_c = cm.bit_length() - 1
    shift_y = n_gy.bit_length() - 1
    for i in range(jpd // jb):
        blk = slice(i * jb, i * jb + jb)
        cells, owner = inc_of[0, :, blk], inc_of[1, :, blk]
        row = lax.shift_right_logical(cells, shift_c)
        oh_row[:, blk] = (cell_rows == row).astype(F32).astype(BF16)
        place = (owner & (n_gy - 1)) * n_gx + lax.shift_right_logical(owner, shift_y)
        oh = (own_rows == place).astype(F32)
        oh_own[:, blk] = oh.astype(BF16)
        before = jnp.dot(oh.astype(BF16), upper, preferred_element_type=F32)
        slot_of[:, blk] = jnp.sum(oh * (before + carry), axis=0, keepdims=True)
        carry = carry + jnp.sum(oh, axis=1, keepdims=True)

    @pl.when(gx < last_x)
    def _():
        row_copy(0, gx).wait_recv()

    @pl.when(gx > 0)
    def _():
        row_copy(1, gx).wait_recv()

    for i in range(2):
        mw[i, rm:nrow, :] = jnp.where(sub_e < 4, row_r[0, i], row_r[1, i])

    step = next(r for r in (24, 40, 88, 8) if nrow % r == 0)

    def around(ref, start):
        rows = pl.ds(pl.multiple_of(start, 8), step)
        above = pl.ds(pl.multiple_of(lax.rem(start + nrow - 8, nrow), 8), 8)
        below = pl.ds(pl.multiple_of(lax.rem(start + step, nrow), 8), 8)
        mid = ref[rows, :]
        tall = jnp.concatenate([ref[above, :], mid, ref[below, :]], axis=0)
        return (
            mid,
            pltpu.roll(tall, 1, 0)[8 : 8 + step],
            pltpu.roll(tall, step + 15, 0)[8 : 8 + step],
            pltpu.roll(mid, 1, 1),
            pltpu.roll(mid, ext - 1, 1),
        )

    col_e = iota((step, ext), 1)
    col_ok = (col_e < cm) | ((col_e < cm + 64) & (gy < last_y)) | ((col_e >= cm + 64) & (gy > 0))

    @pl.loop(0, nrow // step)
    def _(i):
        start = i * step
        mid, *near = around(mw.at[0], start)
        row = start + iota((step, ext), 0)
        ok = (row < rm) | ((row < rm + 4) & (gx < last_x)) | ((row >= rm + 4) & (gx > 0))
        faces = [0.5 * (mid + x) for x in near]
        denom = stiffness + faces[0] + faces[1] + faces[2] + faces[3]
        inv = jnp.where(ok & col_ok, 1.0 / denom, 0.0)
        rows = pl.ds(pl.multiple_of(start, 8), step)
        for n, face in enumerate(faces):
            coef[n, rows, :] = face * inv
        coef[4, rows, :] = inv

    def arrive(f):
        @pl.loop(1, n_gy)
        def _(d):
            msg_arrival(f, lax.rem(gy + d, n_gy)).wait_recv()

        @pl.when(gx < last_x)
        def _():
            cross_copy(0, f, 0).wait_recv()

        @pl.when(gx > 0)
        def _():
            cross_copy(1, f, 0).wait_recv()

        half = cm // 2
        at = blocks * cm
        edges[0] = cross_r[1, f]
        edges[n_gy + 1] = cross_r[0, f]

        @pl.loop(0, n_gy)
        def _(s):
            both = msg_r[f, s, :, at : at + half]
            edges[s + 1, :, 0:half] = both
            edges[s + 1, :, half:cm] = pltpu.roll(both, 4, 0)
            if f == 0:
                packed = msg_r[f, s, :, at + half : at + half + 128]
                edges[s + 1, :, cm:ext] = pltpu.roll(packed, 128 - 8 * blocks, 1)

    def edge_sum(s, lanes):
        sub = iota((8, lanes.stop - lanes.start), 0)
        first = jnp.where(sub < 2, edges[s, :, lanes], 0.0)
        final = jnp.where(sub >= 6, edges[s + 2, :, lanes], 0.0)
        return first, final

    arrive(0)
    whole = slice(0, ext)

    @pl.loop(0, n_gy)
    def _(s):
        first, final = edge_sum(s, whole)
        packed = msg_r[0, s, :, twide : twide + 128]
        for b in range(blocks):
            halo = packed if b == 0 else pltpu.roll(packed, 128 - 8 * b, 1)
            x = jnp.concatenate([msg_r[0, s, :, b * cm : b * cm + cm], halo], axis=1)
            if b == 0:
                x = x + first
            if b == blocks - 1:
                x = x + final
            rows = pl.ds(pl.multiple_of(s * tr + 8 * b, 8), 8)
            load[rows, :] = x * coef[4, rows, :]

    load[rm:nrow, :] = coef[4, rm:nrow, :] * jnp.where(
        sub_e < 4, edges[n_gy] + edges[n_gy + 1], edges[1] + edges[0]
    )

    for src, dst in ((mw.at[1], wbuf.at[0]), (wbuf.at[0], wbuf.at[1]), (wbuf.at[1], wbuf.at[0])):

        @pl.loop(0, nrow // step)
        def _(i):
            start = i * step
            _mid, *near = around(src, start)
            rows = pl.ds(pl.multiple_of(start, 8), step)
            total = load[rows, :]
            for n, x in enumerate(near):
                total = total + coef[n, rows, :] * x
            dst[rows, :] = total

    result = pltpu.make_async_copy(
        wbuf.at[0, pl.ds(0, rm), pl.ds(0, cm)], warp_out, out_sem
    )
    result.start()

    def field_to(j, x):
        hi, lo = split(x.T)
        ft_hi[j * 128 : j * 128 + 128, :] = hi
        ft_lo[j * 128 : j * 128 + 128, :] = lo

    col_rows = iota((cm, jb), 0)

    def at_joints(to_ref):
        @pl.loop(0, jpd // jb)
        def _(i):
            blk = pl.ds(pl.multiple_of(i * jb, jb), jb)
            oh = oh_row[:, blk]
            got = jnp.dot(ft_hi[...], oh, preferred_element_type=F32) + jnp.dot(
                ft_lo[...], oh, preferred_element_type=F32
            )
            col = inc_of[0, :, blk] & (cm - 1)
            to_ref[:, blk] = jnp.sum(
                jnp.where(col_rows == col, got, 0.0), axis=0, keepdims=True
            )

    for j in range(cj):
        lanes = slice(j * 128, j * 128 + 128)
        field_to(j, wbuf[0, 0:rm, lanes] - mw[1, 0:rm, lanes])
    at_joints(theta_of.at[0])

    arrive(1)
    inner = slice(0, cm)

    @pl.loop(0, n_gy)
    def _(s):
        first, final = edge_sum(s, inner)
        for b in range(blocks):
            x = msg_r[1, s, :, b * cm : b * cm + cm]
            if b == 0:
                x = x + first
            if b == blocks - 1:
                x = x + final
            rows = pl.ds(pl.multiple_of(s * tr + 8 * b, 8), 8)
            top[rows, :] = x

    for j in range(cj):
        field_to(j, top[:, j * 128 : j * 128 + 128])
    at_joints(theta_of.at[1])

    kk = iota((128, jb), 0)
    total = jnp.zeros((devices, 128), F32)
    for i in range(jpd // jb):
        blk = slice(i * jb, i * jb + jb)
        rank = slot_of[:, blk].astype(jnp.int32)
        value = jnp.where(kk < cap, theta_of[0, :, blk], theta_of[1, :, blk])
        here = (kk == rank) | (kk == rank + cap)
        value = jnp.where(here, value, (kk == 2 * cap).astype(F32))
        hi, lo = split(value)
        oh = oh_own[:, blk]
        for part in (hi, lo):
            total = total + lax.dot_general(
                oh, part, (((1,), (1,)), ((), ())), preferred_element_type=F32
            )
    for y in range(n_gy):
        out1_s[y] = total[y * n_gx : y * n_gx + n_gx]

    def one_copy(d):
        to = lax.rem(gy + d, n_gy)
        return pltpu.make_async_remote_copy(
            src_ref=out1_s.at[to],
            dst_ref=out1_r.at[gy],
            send_sem=one_ss.at[d],
            recv_sem=one_rs.at[gy],
            device_id=(gx, to),
            device_id_type=MESH,
        )

    def one_arrival(s):
        return pltpu.make_async_remote_copy(
            src_ref=out1_s.at[s],
            dst_ref=out1_r.at[s],
            send_sem=one_ss.at[0],
            recv_sem=one_rs.at[s],
            device_id=(gx, s),
            device_id_type=MESH,
        )

    def two_copy(d):
        to = lax.rem(gx + d, n_gx)
        return pltpu.make_async_remote_copy(
            src_ref=out2_s.at[to],
            dst_ref=out2_r.at[gx],
            send_sem=two_ss.at[d],
            recv_sem=two_rs.at[gx],
            device_id=(to, gy),
            device_id_type=MESH,
        )

    def two_arrival(s):
        return pltpu.make_async_remote_copy(
            src_ref=out2_s.at[s],
            dst_ref=out2_r.at[s],
            send_sem=two_ss.at[0],
            recv_sem=two_rs.at[s],
            device_id=(s, gy),
            device_id_type=MESH,
        )

    @pl.loop(1, n_gy)
    def _(d):
        one_copy(d).start()

    out1_r[gy] = out1_s[gy]

    @pl.loop(1, n_gy)
    def _(d):
        one_arrival(lax.rem(gy + d, n_gy)).wait_recv()

    for x in range(n_gx):
        for y in range(n_gy):
            out2_s[x, y : y + 1, :] = out1_r[y, x : x + 1, :]

    @pl.loop(1, n_gx)
    def _(d):
        two_copy(d).start()

    out2_r[gx] = out2_s[gx]

    @pl.loop(1, n_gx)
    def _(d):
        two_arrival(lax.rem(gx + d, n_gx)).wait_recv()

    for copy in state:
        copy.wait()

    groups = devices // 8
    per = 8 * cap // 128
    flat = out2_r[...].reshape(groups, 8, 128)
    parts = [flat[:, i, :] for i in range(8)]
    counts = [jnp.broadcast_to(p[:, 2 * cap : 2 * cap + 1], (groups, 128)) for p in parts]
    lane = iota((groups, 128), 1)
    for m in range(per):
        inc = theta = jnp.zeros((groups, 128), F32)
        live = jnp.zeros((groups, 128), F32)
        for i in range(8):
            lo, hi = max(i * cap, m * 128), min((i + 1) * cap, m * 128 + 128)
            if lo >= hi:
                continue
            here = (lane >= lo - m * 128) & (lane < hi - m * 128)
            shift = (i * cap - m * 128) % 128
            inc = jnp.where(here, pltpu.roll(parts[i], shift, 1), inc)
            theta = jnp.where(here, pltpu.roll(parts[i], (shift - cap) % 128, 1), theta)
            slot = (lane + (m * 128 - i * cap)).astype(F32)
            live = jnp.where(here, jnp.where(slot < counts[i], 1.0, 0.0), live)
        rows = pl.ds(m, groups, stride=per)
        total0, inelastic, resist = (
            strain_out[0, rows, :],
            strain_out[1, rows, :],
            resist_out[rows, :],
        )
        total_new = total0 + inc
        arrhen = jnp.exp(2.0 - 2.0 / (1.0 + 0.1 * theta * theta))
        arg = shear_mod * (total_new - inelastic) / resist
        hyper = jnp.exp(arg - LN2) - jnp.exp(-arg - LN2)
        rate = rate_scale * arrhen * hyper * jnp.abs(hyper)
        size = jnp.abs(rate)
        target = sat_level * jnp.exp(sat_power * jnp.log(1.0 + size / arrhen))
        resist_new = resist + harden * (1.0 - resist / target) * size
        keep = live > 0.5
        strain_out[0, rows, :] = jnp.where(keep, total_new, total0)
        strain_out[1, rows, :] = jnp.where(keep, inelastic + rate, inelastic)
        resist_out[rows, :] = jnp.where(keep, resist_new, resist)

    result.wait()

    @pl.when(gy > 0)
    def _():
        col_copy(0, gy - 1).wait_send()

    @pl.when(gy < last_y)
    def _():
        col_copy(1, gy + 1).wait_send()

    @pl.when(gx > 0)
    def _():
        row_copy(0, gx - 1).wait_send()

    @pl.when(gx < last_x)
    def _():
        row_copy(1, gx + 1).wait_send()

    for f in range(2):

        @pl.loop(1, n_gy)
        def _(k):
            msg_copy(f, k).wait_send()

        @pl.when(sends_up)
        def _():
            @pl.loop(0, n_gy)
            def _(k):
                cross_copy(0, f, k).wait_send()

        @pl.when(sends_down)
        def _():
            @pl.loop(0, n_gy)
            def _(k):
                cross_copy(1, f, k).wait_send()

    @pl.loop(1, n_gy)
    def _(d):
        one_copy(d).wait_send()

    @pl.loop(1, n_gx)
    def _(d):
        two_copy(d).wait_send()


def solution(mesh):
    n_gx, n_gy = mesh.shape["gx"], mesh.shape["gy"]
    devices = n_gx * n_gy

    def body(
        temp_start,
        heat_input,
        lateral,
        vertical,
        weighting,
        modulus,
        warp_prev,
        joint_cell,
        joint_owner,
        joint_strain,
        joint_resist,
    ):
        layers, tr, columns = temp_start.shape
        rm, cm = modulus.shape
        jpd = joint_cell.shape[0]
        rows = joint_resist.shape[1] // 128
        blocks = tr // 8
        mwide = blocks * cm + cm // 2 + 128
        nrow, ext = rm + 8, cm + 128
        hbm = pl.BlockSpec(memory_space=pl.ANY)
        smem = pl.BlockSpec(memory_space=pltpu.SMEM)
        vmem = pl.BlockSpec(memory_space=pltpu.VMEM)
        dma = pltpu.SemaphoreType.DMA
        scratch = [
            pltpu.VMEM((n_gy, layers, tr, cm), F32),
            pltpu.VMEM((n_gy, layers, tr, cm), F32),
            pltpu.VMEM((2, 3, tr, columns + 256), F32),
            pltpu.VMEM((2, n_gy, 8, mwide), F32),
            pltpu.VMEM((2, n_gy, 8, mwide), F32),
            pltpu.VMEM((2, n_gy, 8, ext), F32),
            pltpu.VMEM((2, 2, 8, ext), F32),
            pltpu.VMEM((2, 2, 8, 128), F32),
            pltpu.VMEM((2, 2, 8, 128), F32),
            pltpu.VMEM((2, 2, 8, ext), F32),
            pltpu.VMEM((2, 2, 8, ext), F32),
            pltpu.VMEM((2, nrow, ext), F32),
            pltpu.VMEM((2, nrow, ext), F32),
            pltpu.VMEM((5, nrow, ext), F32),
            pltpu.VMEM((nrow, ext), F32),
            pltpu.VMEM((n_gy + 2, 8, ext), F32),
            pltpu.VMEM((rm, cm), F32),
            pltpu.VMEM((rm, jpd), BF16),
            pltpu.VMEM((devices, jpd), BF16),
            pltpu.VMEM((1, jpd), F32),
            pltpu.VMEM((cm, rm), BF16),
            pltpu.VMEM((cm, rm), BF16),
            pltpu.VMEM((2, 1, jpd), jnp.int32),
            pltpu.VMEM((2, 1, jpd), F32),
            pltpu.VMEM((n_gy, n_gx, 128), F32),
            pltpu.VMEM((n_gy, n_gx, 128), F32),
            pltpu.VMEM((n_gx, n_gy, 128), F32),
            pltpu.VMEM((n_gx, n_gy, 128), F32),
            dma((2, n_gy)),
            dma((6,)),
            dma,
            dma((2,)),
            dma((2,)),
            dma((2,)),
            dma((2,)),
            dma((2, n_gy)),
            dma((2, n_gy)),
            dma((2, n_gy)),
            dma((2, 2)),
            dma((n_gy,)),
            dma((n_gy,)),
            dma((n_gx,)),
            dma((n_gx,)),
        ]
        warp, strain, resist = pl.pallas_call(
            functools.partial(kernel, n_gx, n_gy),
            out_shape=(
                jax.ShapeDtypeStruct((rm, cm), F32),
                jax.ShapeDtypeStruct((2, rows, 128), F32),
                jax.ShapeDtypeStruct((rows, 128), F32),
            ),
            in_specs=[hbm, hbm, smem, smem, smem, hbm, hbm, hbm, hbm, hbm, hbm],
            out_specs=(hbm, vmem, vmem),
            scratch_shapes=scratch,
            compiler_params=pltpu.CompilerParams(
                collective_id=0, has_side_effects=True, vmem_limit_bytes=56 * 2**20
            ),
        )(
            temp_start,
            heat_input,
            lateral,
            vertical,
            weighting,
            modulus,
            warp_prev,
            joint_cell.reshape(1, jpd),
            joint_owner.reshape(1, jpd),
            joint_strain.reshape(2, rows, 128),
            joint_resist.reshape(rows, 128),
        )
        return (
            warp,
            strain.reshape(joint_strain.shape),
            resist.reshape(joint_resist.shape),
        )

    return jax.shard_map(
        body,
        mesh=mesh,
        in_specs=(
            P(None, ("gx", "gy"), None),
            P(None, ("gx", "gy"), None),
            P(),
            P(),
            P(),
            P("gx", "gy"),
            P("gx", "gy"),
            P(("gx", "gy")),
            P(("gx", "gy"), None),
            P(None, ("gx", "gy"), None),
            P(("gx", "gy"), None),
        ),
        out_specs=(P("gx", "gy"), P(None, ("gx", "gy"), None), P(("gx", "gy"), None)),
        check_vma=False,
    )
```

time: 304 us -> 53 us (0.17)
  local copies, waits for them, and re-layouts: 103 us -> 4.64 us
  starting transfers between devices: 66.1 us -> 0 us
  waiting for transfers between devices: 60.3 us -> 0 us
  other arithmetic: 48.2 us -> 0 us
  Pallas kernels: 0 us -> 47.4 us
  blocking collectives: 23.3 us -> 0 us
    ppermute x20 -> x0, starting transfers between devices: 61.4 us -> none  [the longest x10 36.3 us: with_halo(): before = lax.ppermute(last, axis, up)]
    ppermute x20 -> x0, waiting for transfers between devices: 60.3 us -> none  [the longest x10 46.3 us: with_halo(): before = lax.ppermute(last, axis, up)]
    pallas_call x0 -> x1, Pallas kernels: none -> 47.4 us  [body(): pl.pallas_call(functools.partial(kernel, n_gx, n_gy), out_shape=(jax.Shap...]
    gather x3 -> x0, local copies, waits for them, and re-layouts: 35.5 us -> none  [the longest x2 23.7 us: body(): increment = warp.reshape(-1)[joint_cell] - warp_prev.reshape(-1)[joint_cell]]
    unnamed x46 -> x3, local copies, waits for them, and re-layouts: 32.5 us -> 4.64 us
    all_to_all x1 -> x0, blocking collectives: 23.3 us -> none  [body(): lax.all_to_all(outgoing, ('gx', 'gy'), split_axis=1, concat_axis=1, tiled...]
    all_to_all x2 -> x0, other arithmetic: 14.6 us -> none  [the longest x1 13.7 us: body(): lax.all_to_all(temp, 'gy', split_axis=2, concat_axis=1, tiled=True)]
    all_to_all x3 -> x0, local copies, waits for them, and re-layouts: 13.3 us -> none  [the longest x2 11.9 us: body(): lax.all_to_all(temp, 'gy', split_axis=2, concat_axis=1, tiled=True)]
  transfers between devices with their start and end apart: 21 -> 0, of which waited for: 8 -> 0; matrix products, arithmetic and copies ran while one was open for 25% -> 0% of each run, Pallas kernels for 0% -> 0%
where the time goes in v1:
time: 53 us; the launch traced here: 52.7 us
  Pallas kernels  47.4 us (89%)
  local copies, waits for them, and re-layouts  4.64 us (9%)
  between operations  0.64 us (1%)
    pallas_call x1, Pallas kernels, body(): pl.pallas_call(functools.partial(kernel, n_gx, n_gy), out_shape=(jax.Shap...  47.4 us
    unnamed x3, local copies, waits for them, and re-layouts  4.64 us

profile of v1, /device:TPU:1, one launch (start us, length us, event | category | flops | bytes accessed | tf_op | source)
XLA Modules:
  0.0 52.7 jit_solution(3352788140453622764)
XLA Ops:
  0.6 47.4 %shard_map.130 = (f32[256,512]{1,0:T(8,128)}, f32[2,48,128]{2,1,0:T(8,128)}, f32[48,128]{1,0:T(8,128)}) custom-call(f32[8,32,4096]{2,1,0:T(8,128)} %temp_ref.1, f32[8,32,4096]{2,1,0:T(8,128)} %heat_ref.1, f32[8]{0:T(128)} %lat_ref.1, f32[7]{0:T(128)} %ver_ref.1, f32[8]{0:T(128)} %wei_ref.1, f32[256,512]{1,0:T(8,128)} %mod_ref.1, f32[256,512]{1,0:T(8,128)} %prev_ref.1, ...), custom_call_target="tpu_custom_call" | custom-call | tf_op jit(solution)/shard_map/pallas_call | solution.py:885
  48.0 1.9 %copy.18 = f32[256,512]{1,0:T(8,128)} copy(f32[256,512]{1,0:T(8,128)} %get-tuple-element.15) | data formatting | bytes 1048576
  49.9 1.4 %copy.19 = f32[2,1,6144]{2,1,0:T(1,128)} copy(f32[2,1,6144]{2,1,0:T(1,128)} %bitcast.7) | data formatting | bytes 98304
  51.3 1.3 %copy.20 = f32[1,6144]{1,0:T(1,128)} copy(f32[1,6144]{1,0:T(1,128)} %bitcast.8) | data formatting | bytes 49152

commit v2 on v1

v2 whole, which is shorter than its diff:
```python
import functools

import jax
import jax.numpy as jnp
from jax import lax
from jax.experimental import pallas as pl
from jax.experimental.pallas import tpu as pltpu
from jax.sharding import PartitionSpec as P

MESH = pl.DeviceIdType.MESH
F32 = jnp.float32
BF16 = jnp.bfloat16

stiffness = 0.2
shear_mod = 0.6
rate_scale = 0.5
sat_level = 2.5
sat_power = 0.3
harden = 2.0
LN2 = 0.6931471805599453


def iota(shape, dim):
    return lax.broadcasted_iota(jnp.int32, shape, dim)


def split(x):
    hi = x.astype(BF16)
    return hi, (x - hi.astype(F32)).astype(BF16)


def layer_weights(lat, ver, w):
    n = len(w)

    def add(x, y):
        return y if x is None else x if y is None else x + y

    def mul(x, y):
        return None if x is None else x * y

    def vert(x):
        out = []
        for l in range(n):
            keep = 1.0
            if l < n - 1:
                keep = keep - ver[l]
            if l > 0:
                keep = keep - ver[l - 1]
            total = mul(x[l], keep)
            if l > 0:
                total = add(total, mul(x[l - 1], ver[l - 1]))
            if l < n - 1:
                total = add(total, mul(x[l + 1], ver[l]))
            out.append(total)
        return out

    u = vert(w)
    wd = [mul(x, d) for x, d in zip(w, lat)]
    a0 = vert(u)
    a1 = [add(mul(x, d), y) for x, d, y in zip(u, lat, vert(wd))]
    a2 = [mul(x, d) for x, d in zip(wd, lat)]
    b0 = [add(x, y) for x, y in zip(u, w)]
    return (a0, b0), (a1, wd), (a2, [None] * n)


def kernel(
    n_gx,
    n_gy,
    cap,
    temp_ref,
    heat_ref,
    lat_ref,
    ver_ref,
    wei_ref,
    mod_ref,
    prev_ref,
    cell_ref,
    owner_ref,
    warp_out,
    rows_out,
    tbuf,
    hbuf,
    sums,
    msg_s,
    msg_r,
    cross_s,
    cross_r,
    edge_s,
    edge_r,
    col_s,
    col_r,
    mw,
    wbuf,
    coef,
    load,
    f_hi,
    f_lo,
    oh_col,
    oh_own,
    slot_of,
    owner_of,
    cell_r,
    reply_s,
    reply_r,
    inc_of,
    theta_of,
    out1_s,
    out1_r,
    out2_s,
    load_sem,
    mw_sem,
    aux_sem,
    out_sem,
    col_ss,
    col_rs,
    row_ss,
    row_rs,
    msg_ss,
    msg_rs,
    cross_ss,
    cross_rs,
    edge_ss,
    edge_rs,
    ask_ss,
    ask_rs,
    reply_ss,
    reply_rs,
    one_ss,
    one_rs,
    two_ss,
    two_rs,
):
    layers, tr, columns = temp_ref.shape
    rm, cm = mod_ref.shape
    blocks = tr // 8
    ext = cm + 128
    cj = cm // 128
    devices = n_gx * n_gy
    jpd = cell_ref.shape[1]
    gx, gy = lax.axis_index("gx"), lax.axis_index("gy")
    last_x, last_y = n_gx - 1, n_gy - 1
    base = 16
    below = base + rm

    def remote(src, dst, ss, rs, to):
        return pltpu.make_async_remote_copy(
            src_ref=src,
            dst_ref=dst,
            send_sem=ss,
            recv_sem=rs,
            device_id=to,
            device_id_type=MESH,
        )

    def chunk_of(k):
        return lax.rem(gy + k, n_gy)

    def chunk_copies(k):
        cols = pl.ds(pl.multiple_of(chunk_of(k) * cm, cm), cm)
        return (
            pltpu.make_async_copy(temp_ref.at[:, :, cols], tbuf.at[k], load_sem.at[0, k]),
            pltpu.make_async_copy(heat_ref.at[:, :, cols], hbuf.at[k], load_sem.at[1, k]),
        )

    def mw_copies():
        return [
            pltpu.make_async_copy(
                ref.at[:, pl.ds(j * 128, 128)],
                mw.at[i, j, pl.ds(base, rm), :],
                mw_sem.at[i, j],
            )
            for i, ref in enumerate((mod_ref, prev_ref))
            for j in range(cj)
        ]

    aux = (
        pltpu.make_async_copy(cell_ref, cell_r.at[gy], aux_sem.at[0]),
        pltpu.make_async_copy(owner_ref, owner_of, aux_sem.at[1]),
    )

    @pl.loop(0, 3)
    def _(k):
        for copy in chunk_copies(k):
            copy.start()

    for copy in mw_copies():
        copy.start()
    for copy in aux:
        copy.start()

    @pl.loop(3, n_gy)
    def _(k):
        for copy in chunk_copies(k):
            copy.start()

    @pl.when(gy == last_y)
    def _():
        col_r[0] = jnp.zeros_like(col_r[0])

    @pl.when(gy == 0)
    def _():
        col_r[1] = jnp.zeros_like(col_r[1])

    zero8 = jnp.zeros((8, 128), F32)

    @pl.when(gx == last_x)
    def _():
        for i in range(2):
            for j in range(cj + 1):
                mw[i, j, below : below + 8, :] = zero8
        cross_r[0] = jnp.zeros_like(cross_r[0])
        edge_r[0] = jnp.zeros_like(edge_r[0])

    @pl.when(gx == 0)
    def _():
        for i in range(2):
            for j in range(cj + 1):
                mw[i, j, base - 8 : base, :] = zero8
        cross_r[1] = jnp.zeros_like(cross_r[1])
        edge_r[1] = jnp.zeros_like(edge_r[1])

    barrier = pltpu.get_barrier_semaphore()

    @pl.loop(1, n_gy)
    def _(d):
        pl.semaphore_signal(
            barrier, inc=1, device_id=(gx, lax.rem(gy + d, n_gy)), device_id_type=MESH
        )

    @pl.loop(1, n_gx)
    def _(d):
        pl.semaphore_signal(
            barrier, inc=1, device_id=(lax.rem(gx + d, n_gx), gy), device_id_type=MESH
        )

    @pl.when(gx < last_x)
    def _():
        pl.semaphore_signal(barrier, inc=1, device_id=(gx + 1, 0), device_id_type=MESH)

    @pl.when(gx > 0)
    def _():
        pl.semaphore_signal(
            barrier, inc=1, device_id=(gx - 1, last_y), device_id_type=MESH
        )

    lat = [lat_ref[i] for i in range(layers)]
    ver = [ver_ref[i] for i in range(layers - 1)]
    wei = [wei_ref[i] for i in range(layers)]
    fields = [
        layer_weights(lat, ver, wei),
        layer_weights(lat, ver, [None] * (layers - 1) + [1.0]),
    ]

    zero_cols = jnp.zeros((tr, 128), F32)
    for f in range(2):
        for p in range(3):
            sums[f, p, :, 0:128] = zero_cols
            sums[f, p, :, columns + 128 : columns + 256] = zero_cols
    for j in range(cj + 1):
        for rows in (slice(0, 8), slice(below + 8, below + 16)):
            for ref in (mw.at[0], mw.at[1], wbuf.at[0], wbuf.at[1]):
                ref[j, rows, :] = zero8

    def layer_sums(k):
        for copy in chunk_copies(k):
            copy.wait()
        start = 128 + chunk_of(k) * cm
        for j in range(cj):
            lanes = slice(j * 128, j * 128 + 128)
            acc = [[None] * 3, [None] * 3]
            for l in range(layers):
                t, h = tbuf[k, l, :, lanes], hbuf[k, l, :, lanes]
                for f in range(2):
                    for p in range(3):
                        a, b = fields[f][p]
                        for c, x in ((a[l], t), (b[l], h)):
                            if c is not None:
                                term = c * x
                                acc[f][p] = (
                                    term if acc[f][p] is None else acc[f][p] + term
                                )
            where = pl.ds(pl.multiple_of(start + j * 128, 128), 128)
            for f in range(2):
                for p in range(3):
                    sums[f, p, :, where] = acc[f][p]

    wide = cm + 256
    crow = tr + 8

    def neighbours(x):
        r, c = x.shape
        return (
            pltpu.roll(x, 1, 0)
            + pltpu.roll(x, r - 1, 0)
            + pltpu.roll(x, 1, 1)
            + pltpu.roll(x, c - 1, 1)
            - 4.0 * x
        )

    def contribution(f, c):
        window = pl.ds(pl.multiple_of(c * cm, cm), wide)
        zero = jnp.zeros((8, wide), F32)
        p0, p1, p2 = (
            jnp.concatenate([sums[f, p, :, window], zero], axis=0) for p in range(3)
        )
        q = p1 + neighbours(p2)
        col = c * cm - 128 + iota((crow, wide), 1)
        row = iota((crow, wide), 0)
        panel = (col >= 0) & (col < columns)
        panel = panel & ((row < tr + 4) | (gx > 0) | (gy > 0))
        panel = panel & (
            (row < tr) | (row >= tr + 4) | (gx < last_x) | (gy < last_y)
        )
        q = jnp.where(panel, q, 0.0)
        out = p0 + neighbours(q)
        main = out[:, 128 : 128 + cm]
        lane = iota((crow, 128), 1)
        halo = jnp.where(lane < 64, out[:, 128 + cm :], out[:, 0:128])
        return main, halo

    lane8 = iota((8, 128), 1)
    sub8 = iota((8, 128), 0)
    sub_h = iota((8, cm // 2), 0)
    sub_e = iota((8, ext), 0)
    half = cm // 2
    at = blocks * cm

    def write_message(ref, main, halo):
        for b in range(blocks):
            ref[:, b * cm : b * cm + cm] = main[8 * b : 8 * b + 8]
        edge = main[tr:]
        ref[:, at : at + half] = jnp.where(
            (sub_h < 2) | (sub_h >= 6), edge[:, :half], pltpu.roll(edge[:, half:], 4, 0)
        )
        packed = halo[0:8]
        for b in range(1, blocks + 1):
            here = (lane8 >= 8 * b - 2) & (lane8 < 8 * b + 2)
            packed = jnp.where(
                here, pltpu.roll(halo[8 * b : 8 * b + 8], 8 * b, 1), packed
            )
        ref[:, at + half : at + half + 128] = packed

    def msg_copy(k):
        return remote(
            msg_s.at[k], msg_r.at[gy], msg_ss.at[k], msg_rs.at[gy], (gx, chunk_of(k))
        )

    def msg_arrival(s):
        return remote(msg_s.at[0], msg_r.at[s], msg_ss.at[0], msg_rs.at[s], (gx, s))

    def beyond(side):
        return gx - 1 if side == 0 else gx + 1

    def cross_copy(side, k):
        return remote(
            cross_s.at[k],
            cross_r.at[side],
            cross_ss.at[k],
            cross_rs.at[side],
            (beyond(side), chunk_of(k)),
        )

    def edge_copy(side, k):
        return remote(
            edge_s.at[k],
            edge_r.at[side],
            edge_ss.at[k],
            edge_rs.at[side],
            (beyond(side), chunk_of(k)),
        )

    sends_up = (gy == 0) & (gx > 0)
    sends_down = (gy == last_y) & (gx < last_x)

    def prepare(k, to_ref):
        main, halo = contribution(0, chunk_of(k))
        write_message(to_ref, main, halo)

        @pl.when(sends_up)
        def _():
            block = jnp.concatenate([main, halo], axis=1)
            cross_s[k] = jnp.where(sub_e < 4, block[0:8], block[tr:])

        @pl.when(sends_down)
        def _():
            block = jnp.concatenate([main, halo], axis=1)
            cross_s[k] = jnp.where(sub_e >= 4, block[tr - 8 : tr], block[tr:])

    def send_cross(copy_of, k):
        @pl.when(sends_up)
        def _():
            copy_of(0, k).start()

        @pl.when(sends_down)
        def _():
            copy_of(1, k).start()

    layer_sums(0)
    layer_sums(1)
    layer_sums(2)
    prepare(1, msg_s.at[1])

    greeted = n_gy - 1 + n_gx - 1
    more_up = jnp.where((gy == 0) & (gx > 0), n_gy, 0)
    more_down = jnp.where((gy == last_y) & (gx < last_x), n_gy, 0)
    pl.semaphore_wait(barrier, greeted + more_up + more_down)

    msg_copy(1).start()
    send_cross(cross_copy, 1)

    def ask_copy(d):
        return remote(
            cell_ref, cell_r.at[gy], ask_ss.at[d], ask_rs.at[gy], (gx, chunk_of(d))
        )

    def ask_arrival(s):
        return remote(cell_ref, cell_r.at[s], ask_ss.at[0], ask_rs.at[s], (gx, s))

    for copy in mw_copies():
        copy.wait()
    for i in range(2):
        to_left, to_right = zero8, zero8
        for b in range(rm // 8):
            here = (lane8 >= 4 * b) & (lane8 < 4 * b + 4)
            rows = slice(base + 8 * b, base + 8 * b + 8)
            to_left = jnp.where(here, pltpu.roll(mw[i, 0, rows, :], 4 * b, 1), to_left)
            to_right = jnp.where(
                here,
                pltpu.roll(mw[i, cj - 1, rows, :], (4 * b + 4) % 128, 1),
                to_right,
            )
        col_s[0, i] = to_left
        col_s[1, i] = to_right

    def col_copy(side, to):
        return remote(
            col_s.at[side], col_r.at[side], col_ss.at[side], col_rs.at[side], (gx, to)
        )

    @pl.when(gy > 0)
    def _():
        col_copy(0, gy - 1).start()

    @pl.when(gy < last_y)
    def _():
        col_copy(1, gy + 1).start()

    @pl.loop(1, n_gy)
    def _(d):
        ask_copy(d).start()

    @pl.loop(3, n_gy + 1)
    def _(k):
        @pl.when(k < n_gy)
        def _():
            layer_sums(k)

        prepare(k - 1, msg_s.at[k - 1])
        msg_copy(k - 1).start()
        send_cross(cross_copy, k - 1)

    prepare(0, msg_r.at[gy])
    send_cross(cross_copy, 0)

    @pl.when(gy < last_y)
    def _():
        col_copy(0, gy).wait_recv()

    @pl.when(gy > 0)
    def _():
        col_copy(1, gy).wait_recv()

    for i in range(2):
        right, left = col_r[0, i], col_r[1, i]
        for b in range(rm // 8):
            mw[i, cj, base + 8 * b : base + 8 * b + 8, :] = jnp.where(
                lane8 < 64,
                pltpu.roll(right, (128 - 4 * b) % 128, 1),
                pltpu.roll(left, (256 - 4 * b - 4) % 128, 1),
            )

    def row_copy(side, to):
        src = base if side == 0 else below - 8
        dst = below if side == 0 else base - 8
        return remote(
            mw.at[:, :, pl.ds(src, 8), :],
            mw.at[:, :, pl.ds(dst, 8), :],
            row_ss.at[side],
            row_rs.at[side],
            (to, gy),
        )

    @pl.when(gx > 0)
    def _():
        row_copy(0, gx - 1).start()

    @pl.when(gx < last_x)
    def _():
        row_copy(1, gx + 1).start()

    for copy in aux:
        copy.wait()

    @pl.loop(1, n_gy)
    def _(d):
        ask_arrival(lax.rem(gy + d, n_gy)).wait_recv()

    jb = 256
    shift_c = cm.bit_length() - 1
    shift_y = n_gy.bit_length() - 1
    lane_rows = iota((128, jb), 0)

    def one_hot(rows, at_row):
        return (rows == at_row).astype(F32).astype(BF16)

    def select(table, row_of, cells_ref, to_ref):
        tall = table.shape[0]
        per = tall // cj
        lhs = jnp.concatenate(split(table), axis=1)
        ids = iota((tall, jb), 0)
        for i in range(jpd // jb):
            blk = slice(i * jb, i * jb + jb)
            cells = cells_ref[:, blk]
            row = row_of(lax.shift_right_logical(cells, shift_c))
            block = lax.shift_right_logical(cells & (cm - 1), 7)
            place = jnp.where(row >= 0, block * per + row, -1)
            oh = one_hot(lane_rows, cells & 127)
            got = jnp.dot(
                lhs, jnp.concatenate([oh, oh], axis=0), preferred_element_type=F32
            )
            to_ref[:, blk] = jnp.sum(
                jnp.where(ids == place, got, 0.0), axis=0, keepdims=True
            )

    def stacked(x):
        return jnp.concatenate([x[:, j * 128 : j * 128 + 128] for j in range(cj)], axis=0)

    def near_row(row):
        q = row - gy * tr
        inside = (q >= 0) & (q < tr + 2)
        before = (q < 0) & (q >= -2)
        return jnp.where(inside, q, jnp.where(before, q + crow, -1))

    def reply_copy(k):
        return remote(
            reply_s.at[k],
            reply_r.at[gy],
            reply_ss.at[k],
            reply_rs.at[gy],
            (gx, chunk_of(k)),
        )

    def reply_arrival(s):
        return remote(
            reply_s.at[0], reply_r.at[s], reply_ss.at[0], reply_rs.at[s], (gx, s)
        )

    def answer(k, to_ref):
        main, _halo = contribution(1, chunk_of(k))

        @pl.when(sends_up | sends_down)
        def _():
            edge_s[k] = main[tr:]

        send_cross(edge_copy, k)
        select(stacked(main), near_row, cell_r.at[chunk_of(k)], to_ref)

    @pl.loop(1, n_gy)
    def _(k):
        answer(k, reply_s.at[k])
        reply_copy(k).start()

    answer(0, reply_r.at[gy])

    step = 16
    lane_s = iota((step, 128), 1)

    def around(ref, start):
        rows = pl.ds(pl.multiple_of(start, 8), step)
        mid = [ref[j, rows, :] for j in range(cj + 1)]
        up = [ref[j, pl.ds(start - 1, step), :] for j in range(cj + 1)]
        down = [ref[j, pl.ds(start + 1, step), :] for j in range(cj + 1)]
        to_r = [pltpu.roll(x, 1, 1) for x in mid]
        to_l = [pltpu.roll(x, 127, 1) for x in mid]
        left = [jnp.where(lane_s == 0, to_r[j - 1], to_r[j]) for j in range(cj + 1)]
        right = [
            jnp.where(lane_s == 127, to_l[(j + 1) % (cj + 1)], to_l[j])
            for j in range(cj + 1)
        ]
        return mid, list(zip(up, down, left, right))

    @pl.when(gx < last_x)
    def _():
        row_copy(0, gx).wait_recv()

    @pl.when(gx > 0)
    def _():
        row_copy(1, gx).wait_recv()

    halo_ok = ((lane_s < 64) & (gy < last_y)) | ((lane_s >= 64) & (gy > 0))

    @pl.loop(0, (rm + 16) // step)
    def _(i):
        start = base - 8 + i * step
        rows = pl.ds(pl.multiple_of(start, 8), step)
        mid, near = around(mw.at[0], start)
        row = start + iota((step, 128), 0)
        ok = ((row >= base) | (gx > 0)) & ((row < below) | (gx < last_x))
        for j in range(cj + 1):
            faces = [0.5 * (mid[j] + x) for x in near[j]]
            denom = stiffness + faces[0] + faces[1] + faces[2] + faces[3]
            inv = jnp.where(ok & halo_ok if j == cj else ok, 1.0 / denom, 0.0)
            for n, face in enumerate(faces):
                coef[n, j, rows, :] = face * inv
            coef[4, j, rows, :] = inv

    upper = (iota((jb, jb), 0) < iota((jb, jb), 1)).astype(F32).astype(BF16)
    own_rows = iota((devices, jb), 0)
    col_rows = iota((cm, jb), 0)
    carry = jnp.zeros((devices, 1), F32)
    for i in range(jpd // jb):
        blk = slice(i * jb, i * jb + jb)
        oh_col[:, blk] = one_hot(col_rows, cell_r[gy, :, blk] & (cm - 1))
        owner = owner_of[:, blk]
        place = (owner & (n_gy - 1)) * n_gx + lax.shift_right_logical(owner, shift_y)
        oh = (own_rows == place).astype(F32)
        oh_own[:, blk] = oh.astype(BF16)
        before = jnp.dot(oh.astype(BF16), upper, preferred_element_type=F32)
        slot_of[:, blk] = jnp.sum(oh * (before + carry), axis=0, keepdims=True)
        carry = carry + jnp.sum(oh, axis=1, keepdims=True)

    for j in range(cj + 1):
        for rows in (slice(base - 8, base), slice(below, below + 8)):
            load[j, rows, :] = zero8

    @pl.loop(0, n_gy)
    def _(d):
        s = lax.rem(gy + n_gy - d, n_gy)

        @pl.when(d > 0)
        def _():
            msg_arrival(s).wait_recv()

        packed = msg_r[s, :, at + half : at + half + 128]
        for b in range(blocks):
            rows = pl.ds(pl.multiple_of(base + s * tr + 8 * b, 8), 8)
            for j in range(cj):
                lanes = slice(b * cm + j * 128, b * cm + j * 128 + 128)
                load[j, rows, :] = msg_r[s, :, lanes] * coef[4, j, rows, :]
            halo = packed if b == 0 else pltpu.roll(packed, 128 - 8 * b, 1)
            load[cj, rows, :] = halo * coef[4, cj, rows, :]

    def add_edges(start, keep, parts):
        rows = pl.ds(pl.multiple_of(start, 8), 8)
        for j, x in enumerate(parts):
            load[j, rows, :] = load[j, rows, :] + jnp.where(
                keep, x * coef[4, j, rows, :], 0.0
            )

    for s in range(n_gy):
        both = [msg_r[s, :, at + j * 128 : at + j * 128 + 128] for j in range(cj // 2)]
        parts = both + [pltpu.roll(x, 4, 0) for x in both]
        parts.append(
            pltpu.roll(msg_r[s, :, at + half : at + half + 128], 128 - 8 * blocks, 1)
        )
        add_edges(base + (s + 1) * tr, sub8 < 2, parts)
        add_edges(base + s * tr - 8, sub8 >= 6, parts)

    @pl.when(gx < last_x)
    def _():
        cross_copy(0, 0).wait_recv()
        parts = [cross_r[0, :, j * 128 : j * 128 + 128] for j in range(cj + 1)]
        add_edges(below, sub8 < 2, parts)
        add_edges(below - 8, sub8 >= 6, parts)

    @pl.when(gx > 0)
    def _():
        cross_copy(1, 0).wait_recv()
        parts = [cross_r[1, :, j * 128 : j * 128 + 128] for j in range(cj + 1)]
        add_edges(base, sub8 < 2, parts)
        add_edges(base - 8, sub8 >= 6, parts)

    def swept(src, start, j, near):
        rows = pl.ds(pl.multiple_of(start, 8), step)
        total = load[j, rows, :]
        for n, x in enumerate(near[j]):
            total = total + coef[n, j, rows, :] * x
        return total

    for src, dst in ((mw.at[1], wbuf.at[0]), (wbuf.at[0], wbuf.at[1])):

        @pl.loop(0, (rm + 16) // step)
        def _(i):
            start = base - 8 + i * step
            _mid, near = around(src, start)
            for j in range(cj + 1):
                dst[j, pl.ds(pl.multiple_of(start, 8), step), :] = swept(
                    src, start, j, near
                )

    @pl.loop(0, rm // step)
    def _(i):
        start = base + i * step
        rows = pl.ds(pl.multiple_of(start, 8), step)
        tile_rows = pl.ds(pl.multiple_of(i * step, step), step)
        _mid, near = around(wbuf.at[1], start)
        for j in range(cj):
            lanes = slice(j * 128, j * 128 + 128)
            x = swept(wbuf.at[1], start, j, near)
            wbuf[0, j, rows, :] = x
            hi, lo = split(x - mw[1, j, rows, :])
            f_hi[tile_rows, lanes] = hi
            f_lo[tile_rows, lanes] = lo

    results = [
        pltpu.make_async_copy(
            wbuf.at[0, j, pl.ds(base, rm), :],
            warp_out.at[:, pl.ds(j * 128, 128)],
            out_sem.at[j],
        )
        for j in range(cj)
    ]
    for copy in results:
        copy.start()

    tile_ids = iota((rm, jb), 0)
    for i in range(jpd // jb):
        blk = slice(i * jb, i * jb + jb)
        oh = oh_col[:, blk]
        got = jnp.dot(f_hi[...], oh, preferred_element_type=F32) + jnp.dot(
            f_lo[...], oh, preferred_element_type=F32
        )
        row = lax.shift_right_logical(cell_r[gy, :, blk], shift_c)
        inc_of[:, blk] = jnp.sum(
            jnp.where(tile_ids == row, got, 0.0), axis=0, keepdims=True
        )

    @pl.when(gx < last_x)
    def _():
        edge_copy(0, 0).wait_recv()

    @pl.when(gx > 0)
    def _():
        edge_copy(1, 0).wait_recv()

    def outer_row(row):
        return jnp.where(row < 2, row, jnp.where(row >= rm - 2, row - (rm - 8), -1))

    sub_c = iota((8, cm), 0)
    select(
        stacked(jnp.where(sub_c < 4, edge_r[1], edge_r[0])),
        outer_row,
        cell_r.at[gy],
        theta_of,
    )

    @pl.loop(1, n_gy)
    def _(d):
        reply_arrival(lax.rem(gy + d, n_gy)).wait_recv()

    theta = theta_of[...]
    for s in range(n_gy):
        theta = theta + reply_r[s]
    theta_of[...] = theta

    kk = iota((128, jb), 0)
    total = jnp.zeros((devices, 128), F32)
    for i in range(jpd // jb):
        blk = slice(i * jb, i * jb + jb)
        rank = slot_of[:, blk].astype(jnp.int32)
        value = jnp.where(kk < cap, inc_of[:, blk], theta_of[:, blk])
        here = (kk == rank) | (kk == rank + cap)
        value = jnp.where(here, value, (kk == 2 * cap).astype(F32))
        hi, lo = split(value)
        oh = oh_own[:, blk]
        for part in (hi, lo):
            total = total + lax.dot_general(
                oh, part, (((1,), (1,)), ((), ())), preferred_element_type=F32
            )
    for y in range(n_gy):
        out1_s[y] = total[y * n_gx : y * n_gx + n_gx]

    def one_copy(d):
        to = lax.rem(gy + d, n_gy)
        return remote(
            out1_s.at[to], out1_r.at[gy], one_ss.at[d], one_rs.at[gy], (gx, to)
        )

    def one_arrival(s):
        return remote(out1_s.at[s], out1_r.at[s], one_ss.at[0], one_rs.at[s], (gx, s))

    def two_copy(d):
        to = lax.rem(gx + d, n_gx)
        return remote(
            out2_s.at[to], rows_out.at[gx], two_ss.at[d], two_rs.at[gx], (to, gy)
        )

    def two_arrival(s):
        return remote(out2_s.at[s], rows_out.at[s], two_ss.at[0], two_rs.at[s], (s, gy))

    @pl.loop(1, n_gy)
    def _(d):
        one_copy(d).start()

    out1_r[gy] = out1_s[gy]

    @pl.loop(1, n_gy)
    def _(d):
        one_arrival(lax.rem(gy + d, n_gy)).wait_recv()

    for x in range(n_gx):
        for y in range(n_gy):
            out2_s[x, y : y + 1, :] = out1_r[y, x : x + 1, :]

    @pl.loop(1, n_gx)
    def _(d):
        two_copy(d).start()

    own = pltpu.make_async_copy(out2_s.at[gx], rows_out.at[gx], aux_sem.at[2])
    own.start()

    for copy in results:
        copy.wait()

    @pl.when(gy > 0)
    def _():
        col_copy(0, gy - 1).wait_send()

    @pl.when(gy < last_y)
    def _():
        col_copy(1, gy + 1).wait_send()

    @pl.when(gx > 0)
    def _():
        row_copy(0, gx - 1).wait_send()

    @pl.when(gx < last_x)
    def _():
        row_copy(1, gx + 1).wait_send()

    @pl.loop(1, n_gy)
    def _(k):
        msg_copy(k).wait_send()
        ask_copy(k).wait_send()
        reply_copy(k).wait_send()
        one_copy(k).wait_send()

    for side, sends in ((0, sends_up), (1, sends_down)):

        @pl.when(sends)
        def _():
            @pl.loop(0, n_gy)
            def _(k):
                cross_copy(side, k).wait_send()
                edge_copy(side, k).wait_send()

    own.wait()

    @pl.loop(1, n_gx)
    def _(d):
        two_copy(d).wait_send()

    @pl.loop(1, n_gx)
    def _(d):
        two_arrival(lax.rem(gx + d, n_gx)).wait_recv()


def finish_kernel(
    warp_ref, rows_ref, strain_ref, resist_ref, warp_out, strain_out, resist_out, sem
):
    copy = pltpu.make_async_copy(warp_ref, warp_out, sem)
    copy.start()
    devices = rows_ref.shape[0]
    cap = resist_ref.shape[0] * 128 // devices
    groups = devices // 8
    per = 8 * cap // 128
    parts = [rows_ref[pl.ds(i, groups, stride=8), :] for i in range(8)]
    counts = [jnp.broadcast_to(p[:, 2 * cap : 2 * cap + 1], (groups, 128)) for p in parts]
    lane = iota((groups, 128), 1)
    for m in range(per):
        inc = theta = jnp.zeros((groups, 128), F32)
        live = jnp.zeros((groups, 128), F32)
        for i in range(8):
            lo, hi = max(i * cap, m * 128), min((i + 1) * cap, m * 128 + 128)
            if lo >= hi:
                continue
            here = (lane >= lo - m * 128) & (lane < hi - m * 128)
            shift = (i * cap - m * 128) % 128
            inc = jnp.where(here, pltpu.roll(parts[i], shift, 1), inc)
            theta = jnp.where(here, pltpu.roll(parts[i], (shift - cap) % 128, 1), theta)
            slot = (lane + (m * 128 - i * cap)).astype(F32)
            live = jnp.where(here, jnp.where(slot < counts[i], 1.0, 0.0), live)
        rows = pl.ds(m, groups, stride=per)
        total0, inelastic, resist = (
            strain_ref[0, rows, :],
            strain_ref[1, rows, :],
            resist_ref[rows, :],
        )
        total_new = total0 + inc
        arrhen = jnp.exp(2.0 - 2.0 / (1.0 + 0.1 * theta * theta))
        arg = shear_mod * (total_new - inelastic) / resist
        hyper = jnp.exp(arg - LN2) - jnp.exp(-arg - LN2)
        rate = rate_scale * arrhen * hyper * jnp.abs(hyper)
        size = jnp.abs(rate)
        target = sat_level * jnp.exp(sat_power * jnp.log(1.0 + size / arrhen))
        resist_new = resist + harden * (1.0 - resist / target) * size
        keep = live > 0.5
        strain_out[0, rows, :] = jnp.where(keep, total_new, total0)
        strain_out[1, rows, :] = jnp.where(keep, inelastic + rate, inelastic)
        resist_out[rows, :] = jnp.where(keep, resist_new, resist)
    copy.wait()


def solution(mesh):
    n_gx, n_gy = mesh.shape["gx"], mesh.shape["gy"]
    devices = n_gx * n_gy

    def body(
        temp_start,
        heat_input,
        lateral,
        vertical,
        weighting,
        modulus,
        warp_prev,
        joint_cell,
        joint_owner,
        joint_strain,
        joint_resist,
    ):
        layers, tr, columns = temp_start.shape
        rm, cm = modulus.shape
        jpd = joint_cell.shape[0]
        rows = joint_resist.shape[1] // 128
        blocks = tr // 8
        mwide = blocks * cm + cm // 2 + 128
        ext, cb, tall = cm + 128, cm // 128 + 1, rm + 32
        hbm = pl.BlockSpec(memory_space=pl.ANY)
        smem = pl.BlockSpec(memory_space=pltpu.SMEM)
        vmem = pl.BlockSpec(memory_space=pltpu.VMEM)
        dma = pltpu.SemaphoreType.DMA
        scratch = [
            pltpu.VMEM((n_gy, layers, tr, cm), F32),
            pltpu.VMEM((n_gy, layers, tr, cm), F32),
            pltpu.VMEM((2, 3, tr, columns + 256), F32),
            pltpu.VMEM((n_gy, 8, mwide), F32),
            pltpu.VMEM((n_gy, 8, mwide), F32),
            pltpu.VMEM((n_gy, 8, ext), F32),
            pltpu.VMEM((2, 8, ext), F32),
            pltpu.VMEM((n_gy, 8, cm), F32),
            pltpu.VMEM((2, 8, cm), F32),
            pltpu.VMEM((2, 2, 8, 128), F32),
            pltpu.VMEM((2, 2, 8, 128), F32),
            pltpu.VMEM((2, cb, tall, 128), F32),
            pltpu.VMEM((2, cb, tall, 128), F32),
            pltpu.VMEM((5, cb, tall, 128), F32),
            pltpu.VMEM((cb, tall, 128), F32),
            pltpu.VMEM((rm, cm), BF16),
            pltpu.VMEM((rm, cm), BF16),
            pltpu.VMEM((cm, jpd), BF16),
            pltpu.VMEM((devices, jpd), BF16),
            pltpu.VMEM((1, jpd), F32),
            pltpu.VMEM((1, jpd), jnp.int32),
            pltpu.VMEM((n_gy, 1, jpd), jnp.int32),
            pltpu.VMEM((n_gy, 1, jpd), F32),
            pltpu.VMEM((n_gy, 1, jpd), F32),
            pltpu.VMEM((1, jpd), F32),
            pltpu.VMEM((1, jpd), F32),
            pltpu.VMEM((n_gy, n_gx, 128), F32),
            pltpu.VMEM((n_gy, n_gx, 128), F32),
            pltpu.VMEM((n_gx, n_gy, 128), F32),
            dma((2, n_gy)),
            dma((2, cb - 1)),
            dma((3,)),
            dma((cb - 1,)),
            dma((2,)),
            dma((2,)),
            dma((2,)),
            dma((2,)),
            dma((n_gy,)),
            dma((n_gy,)),
            dma((n_gy,)),
            dma((2,)),
            dma((n_gy,)),
            dma((2,)),
            dma((n_gy,)),
            dma((n_gy,)),
            dma((n_gy,)),
            dma((n_gy,)),
            dma((n_gy,)),
            dma((n_gy,)),
            dma((n_gx,)),
            dma((n_gx,)),
        ]
        warp, sent = pl.pallas_call(
            functools.partial(kernel, n_gx, n_gy, rows * 128 // devices),
            out_shape=(
                jax.ShapeDtypeStruct((rm, cm), F32),
                jax.ShapeDtypeStruct((n_gx, n_gy, 128), F32),
            ),
            in_specs=[hbm, hbm, smem, smem, smem, hbm, hbm, hbm, hbm],
            out_specs=(hbm, hbm),
            scratch_shapes=scratch,
            compiler_params=pltpu.CompilerParams(
                collective_id=0, has_side_effects=True, vmem_limit_bytes=56 * 2**20
            ),
        )(
            temp_start,
            heat_input,
            lateral,
            vertical,
            weighting,
            modulus,
            warp_prev,
            joint_cell.reshape(1, jpd),
            joint_owner.reshape(1, jpd),
        )
        warp, strain, resist = pl.pallas_call(
            finish_kernel,
            out_shape=(
                jax.ShapeDtypeStruct((rm, cm), F32),
                jax.ShapeDtypeStruct((2, rows, 128), F32),
                jax.ShapeDtypeStruct((rows, 128), F32),
            ),
            in_specs=[hbm, vmem, vmem, vmem],
            out_specs=(hbm, vmem, vmem),
            scratch_shapes=[dma],
            compiler_params=pltpu.CompilerParams(vmem_limit_bytes=16 * 2**20),
        )(
            warp,
            sent.reshape(devices, 128),
            joint_strain.reshape(2, rows, 128),
            joint_resist.reshape(rows, 128),
        )
        return (
            warp,
            strain.reshape(joint_strain.shape),
            resist.reshape(joint_resist.shape),
        )

    return jax.shard_map(
        body,
        mesh=mesh,
        in_specs=(
            P(None, ("gx", "gy"), None),
            P(None, ("gx", "gy"), None),
            P(),
            P(),
            P(),
            P("gx", "gy"),
            P("gx", "gy"),
            P(("gx", "gy")),
            P(("gx", "gy"), None),
            P(None, ("gx", "gy"), None),
            P(("gx", "gy"), None),
        ),
        out_specs=(P("gx", "gy"), P(None, ("gx", "gy"), None), P(("gx", "gy"), None)),
        check_vma=False,
    )
```

time: 53 us -> 47.9 us (0.904)
  local copies, waits for them, and re-layouts: 4.64 us -> 1.88 us
  Pallas kernels: 47.4 us -> 45.1 us
    unnamed x3 -> x8, local copies, waits for them, and re-layouts: 4.64 us -> 1.88 us
    pallas_call x1 -> x2, Pallas kernels: 47.4 us -> 45.1 us  [the longest x1 43.6 us: body(): pl.pallas_call(functools.partial(kernel, n_gx, n_gy, rows * 128 // device...]
where the time goes in v2:
time: 47.9 us; the launch traced here: 47.6 us
  Pallas kernels  45.1 us (94%)
  local copies, waits for them, and re-layouts  1.88 us (4%)
  between operations  0.68 us (1%)
    pallas_call x1, Pallas kernels, body(): pl.pallas_call(functools.partial(kernel, n_gx, n_gy, rows * 128 // device...  43.6 us
    unnamed x8, local copies, waits for them, and re-layouts  1.88 us
    pallas_call x1, Pallas kernels, body(): pl.pallas_call(finish_kernel, out_shape=(jax.ShapeDtypeStruct((rm, cm), F...  1.45 us

profile of v2, /device:TPU:1, one launch (start us, length us, event | category | flops | bytes accessed | tf_op | source)
XLA Modules:
  0.0 47.6 jit_solution(17879613190497435133)
XLA Ops:
  0.6 0.0 copy-start.2
  0.6 0.0 copy-start.3
  0.7 43.6 %shard_map.130 = (f32[256,512]{1,0:T(8,128)}, f32[16,8,128]{2,1,0:T(8,128)}) custom-call(f32[8,32,4096]{2,1,0:T(8,128)} %temp_ref.1, f32[8,32,4096]{2,1,0:T(8,128)} %heat_ref.1, f32[8]{0:T(128)} %lat_ref.1, f32[7]{0:T(128)} %ver_ref.1, f32[8]{0:T(128)} %wei_ref.1, f32[256,512]{1,0:T(8,128)} %mod_ref.1, f32[256,512]{1,0:T(8,128)} %prev_ref.1, ...), custom_call_target="tpu_custom_call" | custom-call | tf_op jit(solution)/shard_map/pallas_call | solution.py:995
  44.3 0.0 copy-done.2
  44.3 0.0 copy-done.3
  44.3 0.0 copy-start
  44.3 1.0 %copy-done = f32[256,512]{1,0:T(8,128)S(1)} copy-done((f32[256,512]{1,0:T(8,128)S(1)}, f32[256,512]{1,0:T(8,128)}, u32[]{:S(2)}) %copy-start) | copy-done | bytes 524312
  45.3 0.0 copy-start.1
  45.3 0.8 %copy-done.1 = f32[16,8,128]{2,1,0:T(8,128)S(1)} copy-done((f32[16,8,128]{2,1,0:T(8,128)S(1)}, f32[16,8,128]{2,1,0:T(8,128)}, u32[]{:S(2)}) %copy-start.1) | copy-done | bytes 65560
  46.2 1.5 %shard_map.131 = (f32[256,512]{1,0:T(8,128)}, f32[2,48,128]{2,1,0:T(8,128)}, f32[48,128]{1,0:T(8,128)}) custom-call(f32[256,512]{1,0:T(8,128)S(1)} %copy-done, f32[128,128]{1,0:T(8,128)S(1)} %bitcast.7, f32[2,48,128]{2,1,0:T(8,128)S(1)} %bitcast.8, f32[48,128]{1,0:T(8,128)S(1)} %bitcast.9), custom_call_target="tpu_custom_call" | custom-call | tf_op jit(solution)/shard_map/pallas_call | solution.py:1018
Async XLA Ops:
  0.6 43.6 %copy-start.2 = (f32[2,1,6144]{2,1,0:T(1,128)S(1)}, f32[2,1,6144]{2,1,0:T(1,128)}, u32[]{:S(2)}) copy-start(f32[2,1,6144]{2,1,0:T(1,128)} %param.20) | copy-start | bytes 147460
  0.6 43.6 %copy-start.3 = (f32[1,6144]{1,0:T(1,128)S(1)}, f32[1,6144]{1,0:T(1,128)}, u32[]{:S(2)}) copy-start(f32[1,6144]{1,0:T(1,128)} %param.21) | copy-start | bytes 73732
  44.3 1.0 %copy-start = (f32[256,512]{1,0:T(8,128)S(1)}, f32[256,512]{1,0:T(8,128)}, u32[]{:S(2)}) copy-start(f32[256,512]{1,0:T(8,128)} %get-tuple-element.8.warp_ref) | copy-start | bytes 1572868
  45.3 0.8 %copy-start.1 = (f32[16,8,128]{2,1,0:T(8,128)S(1)}, f32[16,8,128]{2,1,0:T(8,128)}, u32[]{:S(2)}) copy-start(f32[16,8,128]{2,1,0:T(8,128)} %get-tuple-element.9) | copy-start | bytes 196612

commit v3 on v2

--- a/solution.py
+++ b/solution.py
@@ -104,9 +104,7 @@
     reply_r,
     inc_of,
     theta_of,
-    out1_s,
-    out1_r,
-    out2_s,
+    out_s,
     load_sem,
     mw_sem,
     aux_sem,
@@ -125,10 +123,8 @@
     ask_rs,
     reply_ss,
     reply_rs,
-    one_ss,
-    one_rs,
-    two_ss,
-    two_rs,
+    joint_ss,
+    joint_rs,
 ):
     layers, tr, columns = temp_ref.shape
     rm, cm = mod_ref.shape
@@ -221,26 +217,16 @@
 
     barrier = pltpu.get_barrier_semaphore()
 
-    @pl.loop(1, n_gy)
-    def _(d):
+    def device(o):
+        return (lax.div(o, n_gy), lax.rem(o, n_gy))
+
+    def other(m):
+        return lax.rem(gx * n_gy + gy + m, devices)
+
+    @pl.loop(1, devices)
+    def _(m):
         pl.semaphore_signal(
-            barrier, inc=1, device_id=(gx, lax.rem(gy + d, n_gy)), device_id_type=MESH
-        )
-
-    @pl.loop(1, n_gx)
-    def _(d):
-        pl.semaphore_signal(
-            barrier, inc=1, device_id=(lax.rem(gx + d, n_gx), gy), device_id_type=MESH
-        )
-
-    @pl.when(gx < last_x)
-    def _():
-        pl.semaphore_signal(barrier, inc=1, device_id=(gx + 1, 0), device_id_type=MESH)
-
-    @pl.when(gx > 0)
-    def _():
-        pl.semaphore_signal(
-            barrier, inc=1, device_id=(gx - 1, last_y), device_id_type=MESH
+            barrier, inc=1, device_id=device(other(m)), device_id_type=MESH
         )
 
     lat = [lat_ref[i] for i in range(layers)]
@@ -400,10 +386,7 @@
     layer_sums(2)
     prepare(1, msg_s.at[1])
 
-    greeted = n_gy - 1 + n_gx - 1
-    more_up = jnp.where((gy == 0) & (gx > 0), n_gy, 0)
-    more_down = jnp.where((gy == last_y) & (gx < last_x), n_gy, 0)
-    pl.semaphore_wait(barrier, greeted + more_up + more_down)
+    pl.semaphore_wait(barrier, devices - 1)
 
     msg_copy(1).start()
     send_cross(cross_copy, 1)
@@ -507,7 +490,6 @@
 
     jb = 256
     shift_c = cm.bit_length() - 1
-    shift_y = n_gy.bit_length() - 1
     lane_rows = iota((128, jb), 0)
 
     def one_hot(rows, at_row):
@@ -576,7 +558,7 @@
     lane_s = iota((step, 128), 1)
 
     def around(ref, start):
-        rows = pl.ds(pl.multiple_of(start, 8), step)
+        rows = pl.ds(start, step)
         mid = [ref[j, rows, :] for j in range(cj + 1)]
         up = [ref[j, pl.ds(start - 1, step), :] for j in range(cj + 1)]
         down = [ref[j, pl.ds(start + 1, step), :] for j in range(cj + 1)]
@@ -599,10 +581,9 @@
 
     halo_ok = ((lane_s < 64) & (gy < last_y)) | ((lane_s >= 64) & (gy > 0))
 
-    @pl.loop(0, (rm + 16) // step)
-    def _(i):
+    for i in range((rm + 16) // step):
         start = base - 8 + i * step
-        rows = pl.ds(pl.multiple_of(start, 8), step)
+        rows = pl.ds(start, step)
         mid, near = around(mw.at[0], start)
         row = start + iota((step, 128), 0)
         ok = ((row >= base) | (gx > 0)) & ((row < below) | (gx < last_x))
@@ -622,8 +603,7 @@
         blk = slice(i * jb, i * jb + jb)
         oh_col[:, blk] = one_hot(col_rows, cell_r[gy, :, blk] & (cm - 1))
         owner = owner_of[:, blk]
-        place = (owner & (n_gy - 1)) * n_gx + lax.shift_right_logical(owner, shift_y)
-        oh = (own_rows == place).astype(F32)
+        oh = (own_rows == owner).astype(F32)
         oh_own[:, blk] = oh.astype(BF16)
         before = jnp.dot(oh.astype(BF16), upper, preferred_element_type=F32)
         slot_of[:, blk] = jnp.sum(oh * (before + carry), axis=0, keepdims=True)
@@ -651,7 +631,7 @@
             load[cj, rows, :] = halo * coef[4, cj, rows, :]
 
     def add_edges(start, keep, parts):
-        rows = pl.ds(pl.multiple_of(start, 8), 8)
+        rows = pl.ds(start, 8)
         for j, x in enumerate(parts):
             load[j, rows, :] = load[j, rows, :] + jnp.where(
                 keep, x * coef[4, j, rows, :], 0.0
@@ -680,33 +660,28 @@
         add_edges(base, sub8 < 2, parts)
         add_edges(base - 8, sub8 >= 6, parts)
 
-    def swept(src, start, j, near):
-        rows = pl.ds(pl.multiple_of(start, 8), step)
+    def swept(start, j, near):
+        rows = pl.ds(start, step)
         total = load[j, rows, :]
         for n, x in enumerate(near[j]):
             total = total + coef[n, j, rows, :] * x
         return total
 
     for src, dst in ((mw.at[1], wbuf.at[0]), (wbuf.at[0], wbuf.at[1])):
-
-        @pl.loop(0, (rm + 16) // step)
-        def _(i):
+        for i in range((rm + 16) // step):
             start = base - 8 + i * step
             _mid, near = around(src, start)
             for j in range(cj + 1):
-                dst[j, pl.ds(pl.multiple_of(start, 8), step), :] = swept(
-                    src, start, j, near
-                )
-
-    @pl.loop(0, rm // step)
-    def _(i):
+                dst[j, pl.ds(start, step), :] = swept(start, j, near)
+
+    for i in range(rm // step):
         start = base + i * step
-        rows = pl.ds(pl.multiple_of(start, 8), step)
-        tile_rows = pl.ds(pl.multiple_of(i * step, step), step)
+        rows = pl.ds(start, step)
+        tile_rows = pl.ds(i * step, step)
         _mid, near = around(wbuf.at[1], start)
         for j in range(cj):
             lanes = slice(j * 128, j * 128 + 128)
-            x = swept(wbuf.at[1], start, j, near)
+            x = swept(start, j, near)
             wbuf[0, j, rows, :] = x
             hi, lo = split(x - mw[1, j, rows, :])
             f_hi[tile_rows, lanes] = hi
@@ -777,46 +752,20 @@
             total = total + lax.dot_general(
                 oh, part, (((1,), (1,)), ((), ())), preferred_element_type=F32
             )
-    for y in range(n_gy):
-        out1_s[y] = total[y * n_gx : y * n_gx + n_gx]
-
-    def one_copy(d):
-        to = lax.rem(gy + d, n_gy)
-        return remote(
-            out1_s.at[to], out1_r.at[gy], one_ss.at[d], one_rs.at[gy], (gx, to)
-        )
-
-    def one_arrival(s):
-        return remote(out1_s.at[s], out1_r.at[s], one_ss.at[0], one_rs.at[s], (gx, s))
-
-    def two_copy(d):
-        to = lax.rem(gx + d, n_gx)
-        return remote(
-            out2_s.at[to], rows_out.at[gx], two_ss.at[d], two_rs.at[gx], (to, gy)
-        )
-
-    def two_arrival(s):
-        return remote(out2_s.at[s], rows_out.at[s], two_ss.at[0], two_rs.at[s], (s, gy))
-
-    @pl.loop(1, n_gy)
-    def _(d):
-        one_copy(d).start()
-
-    out1_r[gy] = out1_s[gy]
-
-    @pl.loop(1, n_gy)
-    def _(d):
-        one_arrival(lax.rem(gy + d, n_gy)).wait_recv()
-
-    for x in range(n_gx):
-        for y in range(n_gy):
-            out2_s[x, y : y + 1, :] = out1_r[y, x : x + 1, :]
-
-    @pl.loop(1, n_gx)
-    def _(d):
-        two_copy(d).start()
-
-    own = pltpu.make_async_copy(out2_s.at[gx], rows_out.at[gx], aux_sem.at[2])
+    for o in range(devices):
+        out_s[o] = total[o : o + 1]
+
+    me = gx * n_gy + gy
+
+    def joint_copy(m):
+        o = other(m)
+        return remote(out_s.at[o], rows_out.at[me], joint_ss, joint_rs, device(o))
+
+    @pl.loop(1, devices)
+    def _(m):
+        joint_copy(m).start()
+
+    own = pltpu.make_async_copy(out_s.at[me], rows_out.at[me], aux_sem.at[2])
     own.start()
 
     for copy in results:
@@ -843,7 +792,6 @@
         msg_copy(k).wait_send()
         ask_copy(k).wait_send()
         reply_copy(k).wait_send()
-        one_copy(k).wait_send()
 
     for side, sends in ((0, sends_up), (1, sends_down)):
 
@@ -855,21 +803,58 @@
                 edge_copy(side, k).wait_send()
 
     own.wait()
-
-    @pl.loop(1, n_gx)
-    def _(d):
-        two_copy(d).wait_send()
-
-    @pl.loop(1, n_gx)
-    def _(d):
-        two_arrival(lax.rem(gx + d, n_gx)).wait_recv()
+    every = pl.ds(0, devices - 1)
+    all_joints = remote(
+        out_s.at[every], rows_out.at[every], joint_ss, joint_rs, (gx, gy)
+    )
+    all_joints.wait_send()
+    all_joints.wait_recv()
 
 
 def finish_kernel(
-    warp_ref, rows_ref, strain_ref, resist_ref, warp_out, strain_out, resist_out, sem
+    warp_hbm,
+    rows_hbm,
+    strain_hbm,
+    resist_hbm,
+    warp_out,
+    strain_out,
+    resist_out,
+    rows_ref,
+    strain_ref,
+    resist_ref,
+    held,
+    sem,
 ):
-    copy = pltpu.make_async_copy(warp_ref, warp_out, sem)
-    copy.start()
+    loads = [
+        pltpu.make_async_copy(src, dst, sem.at[i])
+        for i, (src, dst) in enumerate(
+            (
+                (rows_hbm, rows_ref),
+                (strain_hbm, strain_ref),
+                (resist_hbm, resist_ref),
+            )
+        )
+    ]
+    for load in loads:
+        load.start()
+    parts_of_warp = 4
+    share = warp_hbm.shape[0] // parts_of_warp
+    warp_rows = [pl.ds(n * share, share) for n in range(parts_of_warp)]
+    into = [
+        pltpu.make_async_copy(warp_hbm.at[r], held.at[r], sem.at[3 + n])
+        for n, r in enumerate(warp_rows)
+    ]
+    out = [
+        pltpu.make_async_copy(held.at[r], warp_out.at[r], sem.at[3 + n])
+        for n, r in enumerate(warp_rows)
+    ]
+    for copy in into:
+        copy.start()
+    for first, then in zip(into, out):
+        first.wait()
+        then.start()
+    for load in loads:
+        load.wait()
     devices = rows_ref.shape[0]
     cap = resist_ref.shape[0] * 128 // devices
     groups = devices // 8
@@ -908,7 +893,8 @@
         strain_out[0, rows, :] = jnp.where(keep, total_new, total0)
         strain_out[1, rows, :] = jnp.where(keep, inelastic + rate, inelastic)
         resist_out[rows, :] = jnp.where(keep, resist_new, resist)
-    copy.wait()
+    for copy in out:
+        copy.wait()
 
 
 def solution(mesh):
@@ -966,9 +952,7 @@
             pltpu.VMEM((n_gy, 1, jpd), F32),
             pltpu.VMEM((1, jpd), F32),
             pltpu.VMEM((1, jpd), F32),
-            pltpu.VMEM((n_gy, n_gx, 128), F32),
-            pltpu.VMEM((n_gy, n_gx, 128), F32),
-            pltpu.VMEM((n_gx, n_gy, 128), F32),
+            pltpu.VMEM((devices, 1, 128), F32),
             dma((2, n_gy)),
             dma((2, cb - 1)),
             dma((3,)),
@@ -987,16 +971,14 @@
             dma((n_gy,)),
             dma((n_gy,)),
             dma((n_gy,)),
-            dma((n_gy,)),
-            dma((n_gy,)),
-            dma((n_gx,)),
-            dma((n_gx,)),
+            dma,
+            dma,
         ]
         warp, sent = pl.pallas_call(
             functools.partial(kernel, n_gx, n_gy, rows * 128 // devices),
             out_shape=(
                 jax.ShapeDtypeStruct((rm, cm), F32),
-                jax.ShapeDtypeStruct((n_gx, n_gy, 128), F32),
+                jax.ShapeDtypeStruct((devices, 1, 128), F32),
             ),
             in_specs=[hbm, hbm, smem, smem, smem, hbm, hbm, hbm, hbm],
             out_specs=(hbm, hbm),
@@ -1022,10 +1004,16 @@
                 jax.ShapeDtypeStruct((2, rows, 128), F32),
                 jax.ShapeDtypeStruct((rows, 128), F32),
             ),
-            in_specs=[hbm, vmem, vmem, vmem],
+            in_specs=[hbm, hbm, hbm, hbm],
             out_specs=(hbm, vmem, vmem),
-            scratch_shapes=[dma],
-            compiler_params=pltpu.CompilerParams(vmem_limit_bytes=16 * 2**20),
+            scratch_shapes=[
+                pltpu.VMEM((devices, 128), F32),
+                pltpu.VMEM((2, rows, 128), F32),
+                pltpu.VMEM((rows, 128), F32),
+                pltpu.VMEM((rm, cm), F32),
+                dma((7,)),
+            ],
+            compiler_params=pltpu.CompilerParams(vmem_limit_bytes=60 * 2**20),
         )(
             warp,
             sent.reshape(devices, 128),

time: 47.9 us -> 41.1 us (0.86)
  Pallas kernels: 45.1 us -> 40.3 us
  local copies, waits for them, and re-layouts: 1.88 us -> 0 us
    pallas_call x1, Pallas kernels: 43.6 us -> 37.8 us  [body(): pl.pallas_call(functools.partial(kernel, n_gx, n_gy, rows * 128 // device...]
    unnamed x8 -> x0, local copies, waits for them, and re-layouts: 1.88 us -> none
    pallas_call x1, Pallas kernels: 1.45 us -> 2.52 us  [body(): pl.pallas_call(finish_kernel, out_shape=(jax.ShapeDtypeStruct((rm, cm), F...]
where the time goes in v3:
time: 41.1 us; the launch traced here: 41 us
  Pallas kernels  40.3 us (98%)
  between operations  0.64 us (2%)
    pallas_call x1, Pallas kernels, body(): pl.pallas_call(functools.partial(kernel, n_gx, n_gy, rows * 128 // device...  37.8 us
    pallas_call x1, Pallas kernels, body(): pl.pallas_call(finish_kernel, out_shape=(jax.ShapeDtypeStruct((rm, cm), F...  2.52 us

profile of v3, /device:TPU:1, one launch (start us, length us, event | category | flops | bytes accessed | tf_op | source)
XLA Modules:
  0.0 41.0 jit_solution(3545190108851025577)
XLA Ops:
  0.6 37.8 %shard_map.130 = (f32[256,512]{1,0:T(8,128)}, f32[128,1,128]{2,1,0:T(1,128)}) custom-call(f32[8,32,4096]{2,1,0:T(8,128)} %temp_ref.1, f32[8,32,4096]{2,1,0:T(8,128)} %heat_ref.1, f32[8]{0:T(128)} %lat_ref.1, f32[7]{0:T(128)} %ver_ref.1, f32[8]{0:T(128)} %wei_ref.1, f32[256,512]{1,0:T(8,128)} %mod_ref.1, f32[256,512]{1,0:T(8,128)} %prev_ref.1, ...), custom_call_target="tpu_custom_call" | custom-call | tf_op jit(solution)/shard_map/pallas_call | solution.py:977
  38.4 2.5 %shard_map.131 = (f32[256,512]{1,0:T(8,128)}, f32[2,48,128]{2,1,0:T(8,128)}, f32[48,128]{1,0:T(8,128)}) custom-call(f32[256,512]{1,0:T(8,128)} %get-tuple-element.8.warp_hbm, f32[128,128]{1,0:T(8,128)} %bitcast.7, f32[2,48,128]{2,1,0:T(8,128)} %bitcast.8, f32[48,128]{1,0:T(8,128)} %bitcast.9), custom_call_target="tpu_custom_call" | custom-call | tf_op jit(solution)/shard_map/pallas_call | solution.py:1000

commit v4 on v3

--- a/solution.py
+++ b/solution.py
@@ -93,8 +93,7 @@
     wbuf,
     coef,
     load,
-    f_hi,
-    f_lo,
+    f_parts,
     oh_col,
     oh_own,
     slot_of,
@@ -217,17 +216,23 @@
 
     barrier = pltpu.get_barrier_semaphore()
 
-    def device(o):
-        return (lax.div(o, n_gy), lax.rem(o, n_gy))
-
-    def other(m):
-        return lax.rem(gx * n_gy + gy + m, devices)
-
-    @pl.loop(1, devices)
-    def _(m):
-        pl.semaphore_signal(
-            barrier, inc=1, device_id=device(other(m)), device_id_type=MESH
-        )
+    def wrapped(i, n):
+        return jnp.where(i >= n, i - n, i)
+
+    def for_others(act):
+        for dy in range(1, n_gy):
+            act((gx, wrapped(gy + dy, n_gy)))
+
+        @pl.loop(1, n_gx)
+        def _(dx):
+            x = wrapped(gx + dx, n_gx)
+            for dy in range(n_gy):
+                act((x, wrapped(gy + dy, n_gy)))
+
+    def greet(to):
+        pl.semaphore_signal(barrier, inc=1, device_id=to, device_id_type=MESH)
+
+    for_others(greet)
 
     lat = [lat_ref[i] for i in range(layers)]
     ver = [ver_ref[i] for i in range(layers - 1)]
@@ -247,9 +252,11 @@
             for ref in (mw.at[0], mw.at[1], wbuf.at[0], wbuf.at[1]):
                 ref[j, rows, :] = zero8
 
-    def layer_sums(k):
+    def await_chunk(k):
         for copy in chunk_copies(k):
             copy.wait()
+
+    def layer_sums(k):
         start = 128 + chunk_of(k) * cm
         for j in range(cj):
             lanes = slice(j * 128, j * 128 + 128)
@@ -362,15 +369,9 @@
         main, halo = contribution(0, chunk_of(k))
         write_message(to_ref, main, halo)
 
-        @pl.when(sends_up)
-        def _():
-            block = jnp.concatenate([main, halo], axis=1)
-            cross_s[k] = jnp.where(sub_e < 4, block[0:8], block[tr:])
-
-        @pl.when(sends_down)
-        def _():
-            block = jnp.concatenate([main, halo], axis=1)
-            cross_s[k] = jnp.where(sub_e >= 4, block[tr - 8 : tr], block[tr:])
+        block = jnp.concatenate([main, halo], axis=1)
+        inner = jnp.where(gy == 0, block[0:8], block[tr - 8 : tr])
+        cross_s[k] = jnp.where((sub_e < 4) == (gy == 0), inner, block[tr:])
 
     def send_cross(copy_of, k):
         @pl.when(sends_up)
@@ -381,9 +382,9 @@
         def _():
             copy_of(1, k).start()
 
-    layer_sums(0)
-    layer_sums(1)
-    layer_sums(2)
+    for k in range(3):
+        await_chunk(k)
+        layer_sums(k)
     prepare(1, msg_s.at[1])
 
     pl.semaphore_wait(barrier, devices - 1)
@@ -432,16 +433,30 @@
     def _(d):
         ask_copy(d).start()
 
-    @pl.loop(3, n_gy + 1)
-    def _(k):
-        @pl.when(k < n_gy)
-        def _():
+    def send_load(k):
+        msg_copy(k).start()
+        send_cross(cross_copy, k)
+
+    pairs = (n_gy - 4) // 2
+
+    @pl.loop(0, pairs)
+    def _(i):
+        ks = (2 * i + 3, 2 * i + 4)
+        for k in ks:
+            await_chunk(k)
+        for k in ks:
             layer_sums(k)
-
+            prepare(k - 1, msg_s.at[k - 1])
+        for k in ks:
+            send_load(k - 1)
+
+    for k in range(2 * pairs + 3, n_gy):
+        await_chunk(k)
+        layer_sums(k)
         prepare(k - 1, msg_s.at[k - 1])
-        msg_copy(k - 1).start()
-        send_cross(cross_copy, k - 1)
-
+        send_load(k - 1)
+    prepare(n_gy - 1, msg_s.at[n_gy - 1])
+    send_load(n_gy - 1)
     prepare(0, msg_r.at[gy])
     send_cross(cross_copy, 0)
 
@@ -537,22 +552,23 @@
             reply_s.at[0], reply_r.at[s], reply_ss.at[0], reply_rs.at[s], (gx, s)
         )
 
-    def answer(k, to_ref):
-        main, _halo = contribution(1, chunk_of(k))
-
-        @pl.when(sends_up | sends_down)
-        def _():
+    group = 4
+
+    @pl.loop(0, n_gy // group)
+    def _(i):
+        ks = [lax.rem(group * i + u + 1, n_gy) for u in range(group)]
+        for k in ks:
+            main, _halo = contribution(1, chunk_of(k))
             edge_s[k] = main[tr:]
-
-        send_cross(edge_copy, k)
-        select(stacked(main), near_row, cell_r.at[chunk_of(k)], to_ref)
-
-    @pl.loop(1, n_gy)
-    def _(k):
-        answer(k, reply_s.at[k])
-        reply_copy(k).start()
-
-    answer(0, reply_r.at[gy])
+            select(stacked(main), near_row, cell_r.at[chunk_of(k)], reply_s.at[k])
+        for k in ks:
+            send_cross(edge_copy, k)
+
+            @pl.when(k > 0)
+            def _():
+                reply_copy(k).start()
+
+    reply_r[gy] = reply_s[0]
 
     step = 16
     lane_s = iota((step, 128), 1)
@@ -684,8 +700,8 @@
             x = swept(start, j, near)
             wbuf[0, j, rows, :] = x
             hi, lo = split(x - mw[1, j, rows, :])
-            f_hi[tile_rows, lanes] = hi
-            f_lo[tile_rows, lanes] = lo
+            f_parts[tile_rows, lanes] = hi
+            f_parts[pl.ds(rm + i * step, step), lanes] = lo
 
     results = [
         pltpu.make_async_copy(
@@ -702,9 +718,8 @@
     for i in range(jpd // jb):
         blk = slice(i * jb, i * jb + jb)
         oh = oh_col[:, blk]
-        got = jnp.dot(f_hi[...], oh, preferred_element_type=F32) + jnp.dot(
-            f_lo[...], oh, preferred_element_type=F32
-        )
+        got = jnp.dot(f_parts[...], oh, preferred_element_type=F32)
+        got = got[:rm] + got[rm:]
         row = lax.shift_right_logical(cell_r[gy, :, blk], shift_c)
         inc_of[:, blk] = jnp.sum(
             jnp.where(tile_ids == row, got, 0.0), axis=0, keepdims=True
@@ -757,13 +772,11 @@
 
     me = gx * n_gy + gy
 
-    def joint_copy(m):
-        o = other(m)
-        return remote(out_s.at[o], rows_out.at[me], joint_ss, joint_rs, device(o))
-
-    @pl.loop(1, devices)
-    def _(m):
-        joint_copy(m).start()
+    def send_joints(to):
+        o = to[0] * n_gy + to[1]
+        remote(out_s.at[o], rows_out.at[me], joint_ss, joint_rs, to).start()
+
+    for_others(send_joints)
 
     own = pltpu.make_async_copy(out_s.at[me], rows_out.at[me], aux_sem.at[2])
     own.start()
@@ -941,8 +954,7 @@
             pltpu.VMEM((2, cb, tall, 128), F32),
             pltpu.VMEM((5, cb, tall, 128), F32),
             pltpu.VMEM((cb, tall, 128), F32),
-            pltpu.VMEM((rm, cm), BF16),
-            pltpu.VMEM((rm, cm), BF16),
+            pltpu.VMEM((2 * rm, cm), BF16),
             pltpu.VMEM((cm, jpd), BF16),
             pltpu.VMEM((devices, jpd), BF16),
             pltpu.VMEM((1, jpd), F32),

time: 41.1 us -> 40 us (0.973)
  Pallas kernels: 40.3 us -> 39.2 us
    pallas_call x1, Pallas kernels: 37.8 us -> 36.7 us  [body(): pl.pallas_call(functools.partial(kernel, n_gx, n_gy, rows * 128 // device...]
where the time goes in v4:
time: 40 us; the launch traced here: 39.9 us
  Pallas kernels  39.2 us (98%)
  between operations  0.64 us (2%)
    pallas_call x1, Pallas kernels, body(): pl.pallas_call(functools.partial(kernel, n_gx, n_gy, rows * 128 // device...  36.7 us
    pallas_call x1, Pallas kernels, body(): pl.pallas_call(finish_kernel, out_shape=(jax.ShapeDtypeStruct((rm, cm), F...  2.52 us

profile of v4, /device:TPU:1, one launch (start us, length us, event | category | flops | bytes accessed | tf_op | source)
XLA Modules:
  0.0 39.9 jit_solution(8965892848574741747)
XLA Ops:
  0.6 36.7 %shard_map.130 = (f32[256,512]{1,0:T(8,128)}, f32[128,1,128]{2,1,0:T(1,128)}) custom-call(f32[8,32,4096]{2,1,0:T(8,128)} %temp_ref.1, f32[8,32,4096]{2,1,0:T(8,128)} %heat_ref.1, f32[8]{0:T(128)} %lat_ref.1, f32[7]{0:T(128)} %ver_ref.1, f32[8]{0:T(128)} %wei_ref.1, f32[256,512]{1,0:T(8,128)} %mod_ref.1, f32[256,512]{1,0:T(8,128)} %prev_ref.1, ...), custom_call_target="tpu_custom_call" | custom-call | tf_op jit(solution)/shard_map/pallas_call | solution.py:989
  37.3 2.5 %shard_map.131 = (f32[256,512]{1,0:T(8,128)}, f32[2,48,128]{2,1,0:T(8,128)}, f32[48,128]{1,0:T(8,128)}) custom-call(f32[256,512]{1,0:T(8,128)} %get-tuple-element.8.warp_hbm, f32[128,128]{1,0:T(8,128)} %bitcast.7, f32[2,48,128]{2,1,0:T(8,128)} %bitcast.8, f32[48,128]{1,0:T(8,128)} %bitcast.9), custom_call_target="tpu_custom_call" | custom-call | tf_op jit(solution)/shard_map/pallas_call | solution.py:1012

commit v5 on v4

--- a/solution.py
+++ b/solution.py
@@ -629,14 +629,7 @@
         for rows in (slice(base - 8, base), slice(below, below + 8)):
             load[j, rows, :] = zero8
 
-    @pl.loop(0, n_gy)
-    def _(d):
-        s = lax.rem(gy + n_gy - d, n_gy)
-
-        @pl.when(d > 0)
-        def _():
-            msg_arrival(s).wait_recv()
-
+    def assemble(s):
         packed = msg_r[s, :, at + half : at + half + 128]
         for b in range(blocks):
             rows = pl.ds(pl.multiple_of(base + s * tr + 8 * b, 8), 8)
@@ -645,6 +638,14 @@
                 load[j, rows, :] = msg_r[s, :, lanes] * coef[4, j, rows, :]
             halo = packed if b == 0 else pltpu.roll(packed, 128 - 8 * b, 1)
             load[cj, rows, :] = halo * coef[4, cj, rows, :]
+
+    for start in range(0, n_gy, group):
+        sources = [lax.rem(gy + n_gy - start - u, n_gy) for u in range(group)]
+        for u, s in enumerate(sources):
+            if start + u > 0:
+                msg_arrival(s).wait_recv()
+        for s in sources:
+            assemble(s)
 
     def add_edges(start, keep, parts):
         rows = pl.ds(start, 8)
@@ -836,6 +837,8 @@
     strain_ref,
     resist_ref,
     held,
+    strain_new,
+    resist_new_ref,
     sem,
 ):
     loads = [
@@ -903,10 +906,16 @@
         target = sat_level * jnp.exp(sat_power * jnp.log(1.0 + size / arrhen))
         resist_new = resist + harden * (1.0 - resist / target) * size
         keep = live > 0.5
-        strain_out[0, rows, :] = jnp.where(keep, total_new, total0)
-        strain_out[1, rows, :] = jnp.where(keep, inelastic + rate, inelastic)
-        resist_out[rows, :] = jnp.where(keep, resist_new, resist)
-    for copy in out:
+        strain_new[0, rows, :] = jnp.where(keep, total_new, total0)
+        strain_new[1, rows, :] = jnp.where(keep, inelastic + rate, inelastic)
+        resist_new_ref[rows, :] = jnp.where(keep, resist_new, resist)
+    small = [
+        pltpu.make_async_copy(strain_new, strain_out, sem.at[1]),
+        pltpu.make_async_copy(resist_new_ref, resist_out, sem.at[2]),
+    ]
+    for copy in small:
+        copy.start()
+    for copy in out + small:
         copy.wait()
 
 
@@ -936,7 +945,6 @@
         ext, cb, tall = cm + 128, cm // 128 + 1, rm + 32
         hbm = pl.BlockSpec(memory_space=pl.ANY)
         smem = pl.BlockSpec(memory_space=pltpu.SMEM)
-        vmem = pl.BlockSpec(memory_space=pltpu.VMEM)
         dma = pltpu.SemaphoreType.DMA
         scratch = [
             pltpu.VMEM((n_gy, layers, tr, cm), F32),
@@ -1017,12 +1025,14 @@
                 jax.ShapeDtypeStruct((rows, 128), F32),
             ),
             in_specs=[hbm, hbm, hbm, hbm],
-            out_specs=(hbm, vmem, vmem),
+            out_specs=(hbm, hbm, hbm),
             scratch_shapes=[
                 pltpu.VMEM((devices, 128), F32),
                 pltpu.VMEM((2, rows, 128), F32),
                 pltpu.VMEM((rows, 128), F32),
                 pltpu.VMEM((rm, cm), F32),
+                pltpu.VMEM((2, rows, 128), F32),
+                pltpu.VMEM((rows, 128), F32),
                 dma((7,)),
             ],
             compiler_params=pltpu.CompilerParams(vmem_limit_bytes=60 * 2**20),

time: 40 us -> 39.5 us (0.988)
  Pallas kernels: 39.2 us -> 38.7 us
    pallas_call x1, Pallas kernels: 2.52 us -> 2 us  [body(): pl.pallas_call(finish_kernel, out_shape=(jax.ShapeDtypeStruct((rm, cm), F...]
where the time goes in v5:
time: 39.5 us; the launch traced here: 39.3 us
  Pallas kernels  38.7 us (98%)
  between operations  0.64 us (2%)
    pallas_call x1, Pallas kernels, body(): pl.pallas_call(functools.partial(kernel, n_gx, n_gy, rows * 128 // device...  36.7 us
    pallas_call x1, Pallas kernels, body(): pl.pallas_call(finish_kernel, out_shape=(jax.ShapeDtypeStruct((rm, cm), F...  2 us

profile of v5, /device:TPU:1, one launch (start us, length us, event | category | flops | bytes accessed | tf_op | source)
XLA Modules:
  0.0 39.3 jit_solution(1231186528677555896)
XLA Ops:
  0.6 36.7 %shard_map.130 = (f32[256,512]{1,0:T(8,128)}, f32[128,1,128]{2,1,0:T(1,128)}) custom-call(f32[8,32,4096]{2,1,0:T(8,128)} %temp_ref.1, f32[8,32,4096]{2,1,0:T(8,128)} %heat_ref.1, f32[8]{0:T(128)} %lat_ref.1, f32[7]{0:T(128)} %ver_ref.1, f32[8]{0:T(128)} %wei_ref.1, f32[256,512]{1,0:T(8,128)} %mod_ref.1, f32[256,512]{1,0:T(8,128)} %prev_ref.1, ...), custom_call_target="tpu_custom_call" | custom-call | tf_op jit(solution)/shard_map/pallas_call | solution.py:997
  37.3 2.0 %shard_map.131 = (f32[256,512]{1,0:T(8,128)}, f32[2,48,128]{2,1,0:T(8,128)}, f32[48,128]{1,0:T(8,128)}) custom-call(f32[256,512]{1,0:T(8,128)} %get-tuple-element.8.warp_hbm, f32[128,128]{1,0:T(8,128)} %bitcast.7, f32[2,48,128]{2,1,0:T(8,128)} %bitcast.8, f32[48,128]{1,0:T(8,128)} %bitcast.9), custom_call_target="tpu_custom_call" | custom-call | tf_op jit(solution)/shard_map/pallas_call | solution.py:1020
